TPU v7x, 512 devices: a whole 4x4x16 slice. The times are simulated.
512 devices in a mesh: dp: 32 (over z, core), section: 8 (over x_hi, y), mp: 2 (over x_lo).
Axes of the slice: x: 4 (x_hi: 2, x_lo: 2; x = x_hi * 2 + x_lo), y: 4, z: 16, core: 2. Of those that a mesh axis runs over, the one named last changes fastest.
Arguments:
- neighbour_ids: int32 [64, 256], P('dp'), may hold values from 0 to 63999, as said below
- embed_table: bfloat16 [64000, 896], P(('dp', 'mp')), may hold values from -200 to 200
- enc_gain: float32 [896], replicated, may hold values from 0.1 to 1.9
- kv_weight: bfloat16 [8, 896, 2, 2048], P('section', 'dp', None, 'mp'), may hold values from -0.1875 to 0.1875
- queries: bfloat16 [8, 4096, 2048], P('section', 'dp', 'mp'), may hold values from -70 to 70
- grad_out: bfloat16 [8, 4096, 2048], P('section', 'dp', 'mp'), may hold values from -6 to 6
Outputs:
- attn_out: bfloat16 [8, 4096, 2048], P('section', 'dp', 'mp')
- grad_queries: bfloat16 [8, 4096, 2048], P('section', 'dp', 'mp')
- grad_kv_weight: bfloat16 [8, 896, 2, 2048], P('section', 'dp', None, 'mp')
- grad_encodings: bfloat16 [64, 256, 896], P('dp')
Inputs may be any that keep to these rules, and one draw needn't show every extreme that they name: `neighbour_ids`: the ids of the 2 rows of one index of dp fall at most 12 times into one block of 1000 consecutive ids, and some block receives exactly 12 of them.
All inputs are finite; a program needn't handle non-finite values.
Results may differ from a plain program's by a relative error of at most 0.03.
The roundings to bfloat16 on the way count: a program that leaves them out, or rounds other values in their place, can miss the bound.
Values may be sent and summed in bfloat16 or wider, within the bound.
A program may use at most 64 MiB of HBM per device.

v0:
```python
import math

import jax
import jax.numpy as jnp
from jax import lax
from jax.sharding import PartitionSpec as P

HEAD_DIM = 128
SPAN = 64


def encode_rows(neighbour_ids, embed_table, enc_gain):
    owner_count = lax.axis_size(("dp", "mp"))
    owner_rows = embed_table.shape[0]
    id_flat = neighbour_ids.reshape(-1)
    total_ids = id_flat.shape[0]
    capacity = 3 * total_ids // (2 * owner_count)
    owner_of = id_flat // owner_rows
    offset_of = id_flat - owner_of * owner_rows
    matches = (owner_of[:, None] == jnp.arange(owner_count, dtype=jnp.int32)[None, :]).astype(
        jnp.int32
    )
    slot_of = jnp.sum(jnp.cumsum(matches, axis=0) * matches, axis=1) - 1
    target = owner_of * capacity + slot_of
    request = jnp.zeros((owner_count * capacity,), jnp.int32).at[target].set(offset_of)
    request = request.reshape(owner_count, capacity)
    found = jnp.take(
        embed_table,
        lax.all_to_all(request, ("dp", "mp"), split_axis=0, concat_axis=0, tiled=True),
        axis=0,
    )
    answers = lax.all_to_all(found, ("dp", "mp"), split_axis=0, concat_axis=0, tiled=True)
    looked = answers.reshape(owner_count * capacity, embed_table.shape[1])[target].astype(
        jnp.float32
    )
    mean_square = jnp.mean(looked * looked, axis=-1, keepdims=True)
    normed = looked * lax.rsqrt(mean_square + 1e-06) * enc_gain
    return normed.astype(jnp.bfloat16).reshape(neighbour_ids.shape + (embed_table.shape[1],))


def body(neighbour_ids, embed_table, enc_gain, kv_weight, queries, grad_out):
    encoded = encode_rows(neighbour_ids, embed_table, enc_gain)
    span_count, nbr_rows, enc_width = encoded.shape
    local_width = kv_weight.shape[3]
    head_count = local_width // HEAD_DIM
    inv_root = 1.0 / math.sqrt(HEAD_DIM)
    weight = lax.all_gather(kv_weight, "dp", axis=1, tiled=True)[0]
    keyval = jnp.einsum(
        "cre,eka->crka", encoded, weight, preferred_element_type=jnp.float32
    ).astype(jnp.bfloat16)
    key_heads = keyval[:, :, 0].reshape(span_count, nbr_rows, head_count, HEAD_DIM)
    value_heads = keyval[:, :, 1].reshape(span_count, nbr_rows, head_count, HEAD_DIM)
    query_heads = queries[0].reshape(span_count, SPAN, head_count, HEAD_DIM)
    grad_heads = grad_out[0].reshape(span_count, SPAN, head_count, HEAD_DIM)
    scores = (
        jnp.einsum("cqhd,crhd->chqr", query_heads, key_heads, preferred_element_type=jnp.float32)
        * inv_root
    )
    score_top = jnp.max(scores, axis=-1, keepdims=True)
    expo_val = jnp.exp(scores - score_top)
    prob_f = expo_val / jnp.sum(expo_val, axis=-1, keepdims=True)
    prob_b = prob_f.astype(jnp.bfloat16)
    attended = jnp.einsum(
        "chqr,crhd->cqhd", prob_b, value_heads, preferred_element_type=jnp.float32
    ).astype(jnp.bfloat16)
    grad_prob = jnp.einsum(
        "cqhd,crhd->chqr", grad_heads, value_heads, preferred_element_type=jnp.float32
    )
    inner = jnp.sum(grad_prob * prob_f, axis=-1, keepdims=True)
    grad_score = (prob_f * (grad_prob - inner) * inv_root).astype(jnp.bfloat16)
    grad_query = jnp.einsum(
        "chqr,crhd->cqhd", grad_score, key_heads, preferred_element_type=jnp.float32
    ).astype(jnp.bfloat16)
    grad_key = jnp.einsum(
        "chqr,cqhd->crhd", grad_score, query_heads, preferred_element_type=jnp.float32
    ).astype(jnp.bfloat16)
    grad_value = jnp.einsum(
        "chqr,cqhd->crhd", prob_b, grad_heads, preferred_element_type=jnp.float32
    ).astype(jnp.bfloat16)
    grad_kv = jnp.stack(
        [
            grad_key.reshape(span_count, nbr_rows, local_width),
            grad_value.reshape(span_count, nbr_rows, local_width),
        ],
        axis=2,
    )
    weight_share = lax.psum_scatter(
        jnp.einsum("cre,crka->eka", encoded, grad_kv, preferred_element_type=jnp.float32).astype(
            jnp.bfloat16
        ),
        "dp",
        scatter_dimension=0,
        tiled=True,
    )
    enc_term = jnp.einsum("crka,eka->cre", grad_kv, weight, preferred_element_type=jnp.float32)
    summed = lax.psum(enc_term, ("section", "mp")).astype(jnp.bfloat16)
    token_rows = span_count * SPAN
    return (
        attended.reshape(1, token_rows, local_width),
        grad_query.reshape(1, token_rows, local_width),
        weight_share[None],
        summed,
    )


def solution(mesh):
    in_specs = (
        P("dp", None),
        P(("dp", "mp"), None),
        P(),
        P("section", "dp", None, "mp"),
        P("section", "dp", "mp"),
        P("section", "dp", "mp"),
    )
    out_specs = (
        P("section", "dp", "mp"),
        P("section", "dp", "mp"),
        P("section", "dp", None, "mp"),
        P("dp", None, None),
    )
    return jax.shard_map(body, mesh=mesh, in_specs=in_specs, out_specs=out_specs, check_vma=False)
```

profile of v0, /device:TPU:6, one launch (start us, length us, event | category | flops | bytes accessed | tf_op | source)
XLA Modules:
  0.0 423.1 jit_solution(15302201534400584362)
XLA Ops:
  7.2 0.7 all-gather.2.cloned.1.call-update
  7.9 0.7 fusion.64
  8.6 0.7 compare_and_fusion.1
  9.3 0.7 fusion.63
  10.0 0.7 broadcast_divide_fusion.1
  10.7 0.7 copy.65
  11.5 1.2 reduce-window.6
  12.7 0.2 slice_reduce_fusion
  12.9 0.1 fusion.44
  13.1 2.4 scatter_custom_fusion
  15.6 29.6 %all_to_all.20 = s32[64,1,12]{2,1,0:T(1,128)S(1)} all-to-all(s32[64,1,12]{2,1,0:T(1,128)S(1)} %bitcast.126), channel_id=1, replica_groups=mesh['dp'=32,'section'=8,'mp'=2] {'dp','mp'}, dimensions={0} | all-to-all | bytes 6144 | tf_op jit(solution)/shard_map/all_to_all | solution.py:29
  45.4 2.8 gather_fusion
  48.2 1.4 reshape.246
  49.7 3.1 broadcast_select_fusion
  52.7 6.4 %all-to-all-start.1 = ((bf16[64,12,896]{2,1,0:T(8,128)(2,1)}), bf16[64,12,896]{2,1,0:T(8,128)(2,1)}, u32[]{:S(2)}, u32[]{:S(2)}) async-start(bf16[64,12,896]{2,1,0:T(8,128)(2,1)} %broadcast_select_fusion), calls=%async_computation.1 | async-start | bytes 3670016 | tf_op jit(solution)/shard_map/all_to_all | solution.py:32
  59.1 0.2 all-reduce.4.cloned.1.call-start
  59.4 0.8 copy.69
  60.2 1.3 dynamic-slice
  62.1 93.3 %all-to-all-done.1 = bf16[64,12,896]{2,1,0:T(8,128)(2,1)} async-done(((bf16[64,12,896]{2,1,0:T(8,128)(2,1)}), bf16[64,12,896]{2,1,0:T(8,128)(2,1)}, u32[]{:S(2)}, u32[]{:S(2)}) %all-to-all-start.1) | async-done | bytes 1376288 | tf_op jit(solution)/shard_map/all_to_all | solution.py:32
  155.5 2.4 reshape.241
  157.9 2.7 gather_fusion.1
  160.6 1.5 multiply_reduce_fusion
  162.1 2.5 copy.53
  164.7 1.2 multiply_convert_fusion.1
  165.9 4.7 %fusion.8 = bf16[2,256,2,1024]{3,1,2,0:T(8,128)(2,1)S(1)} fusion(bf16[2,256,896,1]{2,1,3,0:T(8,128)(2,1)} %bitcast.121, bf16[1,896,2,1024]{3,2,0,1:T(2,128)(2,1)} %all-gather.2.cloned.1.call-done), kind=kOutput, calls=%fused_computation.13 | convolution fusion | flops 1880096768 | bytes 6684672 | tf_op jit(solution)/shard_map/cre,eka->crka/dot_general | solution.py:48
  170.6 0.2 fusion.57
  170.8 0.3 copy.66
  171.1 0.3 copy.68
  171.4 0.5 fusion.19
  171.9 0.2 copy-done.3
  172.1 1.3 fusion.58
  173.4 1.4 convolution_bitcast_fusion
  174.9 4.6 %convolution_convert_fusion = bf16[2,8,256,128]{2,3,1,0:T(8,128)(2,1)} fusion(bf16[2,64,8,128]{3,2,1,0:T(8,128)(2,1)S(1)} %bitcast.118, f32[2,8,64]{2,1,0:T(8,128)S(1)} %get-tuple-element.16, f32[2,8,64,256]{3,2,1,0:T(8,128)} %copy-done.2), kind=kOutput, calls=%fused_computation.20 | convolution fusion | flops 68420864 | bytes 2363392 | tf_op jit(solution)/shard_map/chqr,cqhd->crhd/dot_general | solution.py:77
  179.5 8.9 %convolution_convert_fusion.1 = bf16[2,8,256,128]{2,3,1,0:T(8,128)(2,1)} fusion(f32[2,8,64,256]{3,2,1,0:T(8,128)} %convolution_bitcast_fusion, bf16[2,64,8,128]{3,2,1,0:T(8,128)(2,1)S(1)} %bitcast.116, f32[2,8,64,256]{3,2,1,0:T(8,128)} %get-tuple-element.17, f32[2,8,64]{2,1,0:T(8,128)S(1)} %get-tuple-element.16), kind=kOutput, calls=%fused_computation.21 | convolution fusion | flops 69469440 | bytes 3411968 | tf_op jit(solution)/shard_map/chqr,cqhd->crhd/dot_general | solution.py:74
  188.4 2.3 copy.56
  190.7 2.3 copy.57
  193.0 4.2 bitcast_convert_fusion
  197.2 5.6 %copy.58 = bf16[896,2,1024]{2,1,0:T(2,128)(2,1)} copy(bf16[896,2,1024]{2,0,1:T(8,128)(2,1)S(1)} %bitcast_convert_fusion) | data formatting | bytes 7340032 | tf_op jit(solution)/shard_map/convert_element_type | solution.py:88
  202.8 7.9 %fusion.22 = bf16[2,64,8,128]{3,1,2,0:T(8,128)(2,1)S(1)} fusion(f32[2,8,64,256]{3,2,1,0:T(8,128)} %convolution_bitcast_fusion, bf16[2,256,8,128]{3,2,1,0:T(8,128)(2,1)} %bitcast.112, f32[2,8,64,256]{3,2,1,0:T(8,128)} %get-tuple-element.17, f32[2,8,64]{2,1,0:T(8,128)S(1)} %get-tuple-element.16), kind=kOutput, calls=%fused_computation.33 | convolution fusion | flops 69076224 | bytes 3411968 | tf_op jit(solution)/shard_map/chqr,crhd->cqhd/dot_general | solution.py:71
  210.7 0.2 copy.52
  210.9 0.8 reshape.243
  211.7 6.4 %fusion.11 = f32[2,256,896]{2,1,0:T(8,128)} fusion(bf16[1,896,2,1024]{3,2,0,1:T(2,128)(2,1)} %all-gather.2.cloned.1.call-done, bf16[2,256,1,1024]{3,1,0,2:T(8,128)(2,1)} %copy.57, bf16[2,256,1,1024]{3,1,0,2:T(8,128)(2,1)} %copy.56), kind=kOutput, calls=%fused_computation.18 | convolution fusion | flops 1880096768 | bytes 7602176 | tf_op jit(solution)/shard_map/crka,eka->cre/dot_general | solution.py:95
  218.1 3.4 fusion.21
  221.5 0.2 copy.48
  221.7 0.8 reshape.242
  222.5 87.0 %all-reduce.5 = bf16[2,256,896]{2,1,0:T(8,128)(2,1)} all-reduce(f32[2,256,896]{2,1,0:T(8,128)} %fusion.11), channel_id=1, replica_groups=mesh['dp'=32,'section'=8,'mp'=2] {'section','mp'}, use_global_device_ids=true, to_apply=%region_9.10 | all-reduce | flops 458752 | bytes 2752512 | tf_op jit(solution)/shard_map/psum | solution.py:96
  309.5 105.2 %all-reduce.4.cloned.1.call-done = bf16[896,2,1024]{2,1,0:T(2,128)(2,1)} async-done(((bf16[896,2,1024]{2,1,0:T(2,128)(2,1)}), bf16[896,2,1024]{2,1,0:T(2,128)(2,1)}) %all-reduce.4.cloned.1.call-update) | async-done | bytes 3670032
  414.7 1.6 dynamic-slice_bitcast_fusion
  (38 shorter events, 0.5 us)
Async XLA Ops:
  7.2 38.2 %copy-start = (bf16[1000,896]{1,0:T(8,128)(2,1)S(1)}, bf16[1000,896]{1,0:T(8,128)(2,1)}, u32[]{:S(2)}) copy-start(bf16[1000,896]{1,0:T(8,128)(2,1)} %param.7) | copy-start | bytes 5376004
  7.2 158.7 %all-gather.2.cloned.1.call-start = ((), (), s32[]{:S(2)}) async-start(), calls=%async_computation.2 | async-start | bytes 3784704 | tf_op jit(solution)/shard_map/all_gather | solution.py:47
  52.7 6.6 %copy-start.5 = (bf16[1,128,1024]{2,1,0:T(8,128)(2,1)S(1)}, bf16[1,128,1024]{2,1,0:T(8,128)(2,1)}, u32[]{:S(2)}) copy-start(bf16[1,128,1024]{2,1,0:T(8,128)(2,1)} %param.10) | copy-start | bytes 786436
  52.7 6.7 %copy-start.6 = (bf16[1,128,1024]{2,1,0:T(8,128)(2,1)S(1)}, bf16[1,128,1024]{2,1,0:T(8,128)(2,1)}, u32[]{:S(2)}) copy-start(bf16[1,128,1024]{2,1,0:T(8,128)(2,1)} %param.11) | copy-start | bytes 786436
  52.7 102.7 %all-to-all-start.1 = ((bf16[64,12,896]{2,1,0:T(8,128)(2,1)}), bf16[64,12,896]{2,1,0:T(8,128)(2,1)}, u32[]{:S(2)}, u32[]{:S(2)}) async-start(bf16[64,12,896]{2,1,0:T(8,128)(2,1)} %broadcast_select_fusion), calls=%async_computation.1 | async-start | bytes 3670016 | tf_op jit(solution)/shard_map/all_to_all | solution.py:32
  59.1 355.5 %all-reduce.4.cloned.1.call-start = ((), (), s32[]{:S(2)}) async-start(), calls=%async_computation.3 | async-start | bytes 7340032
  160.6 4.0 copy-start.1
  160.6 4.0 copy-start.7
  171.1 1.0 copy-start.3
  171.4 2.1 copy-start.4
  172.1 2.8 copy-start.2
Sparse Core Ops, SparseCore 0:
  10.1 102.2 all-gather.1
  202.9 211.7 all-reduce.3
where the time goes:
time: 425 us; the launch traced here: 423 us
  waiting for transfers between devices  199 us (47%)
  blocking collectives  117 us (28%)
  matrix products  42.1 us (10%)
  local copies, waits for them, and re-layouts  32.3 us (8%)
  between operations  14.9 us (4%)
  other arithmetic  11.3 us (3%)
  starting transfers between devices  6.66 us (2%)
    unnamed x3, waiting for transfers between devices  106 us
    all_to_all x1, waiting for transfers between devices, encode_rows(): lax.all_to_all(found, ('dp', 'mp'), split_axis=0, concat_axis=0, tiled=True)  93.3 us
    psum x1, blocking collectives, body(): summed = lax.psum(enc_term, ('section', 'mp')).astype(jnp.bfloat16)  87 us
    all_to_all x1, blocking collectives, encode_rows(): lax.all_to_all(request, ('dp', 'mp'), split_axis=0, concat_axis=0, tiled=...  29.6 us
    dot_general x1, matrix products, body(): jnp.einsum('chqr,cqhd->crhd', grad_score, query_heads, preferred_element_...  8.91 us
  transfers between devices with their start and end apart: 3, of which 2 were waited for; matrix products, arithmetic and copies ran while one was open for 11% of the time, Pallas kernels for 0%

commit v1 on v0

v1 whole, which is shorter than its diff:
```python
import functools
import math

import jax
import jax.numpy as jnp
from jax import lax
from jax.experimental import pallas as pl
from jax.experimental.pallas import tpu as pltpu
from jax.sharding import PartitionSpec as P

HEAD_DIM = 128
SPAN = 64
PACK = 16
MESH = pl.DeviceIdType.MESH
F32 = jnp.float32
BF16 = jnp.bfloat16
NT = (((1,), (1,)), ((), ()))
TN = (((0,), (0,)), ((), ()))


def dot(a, b, dims=(((1,), (0,)), ((), ()))):
    return lax.dot_general(a, b, dims, preferred_element_type=F32)


def iota(shape, axis):
    return lax.broadcasted_iota(jnp.int32, shape, axis)


def kernel(
    n_dp, n_sec, n_mp, cap, e_rows,
    ids_ref, table_ref, gain_ref, w_ref, q_ref, g_ref,
    attn_ref, gq_ref, wg_ref, genc_ref,
    ids_buf, pack_buf, land_buf, rows_buf, spread, pad_mat, place,
    enc_buf, enct_buf, wbuf, gbuf, eacc, pbuf, sib, sbuf, rbuf,
    esend, eland, gall,
    ids_send, ids_recv, pack_send, pack_recv, row_send, row_recv,
    ring_send, ring_recv, twin_send, twin_recv,
    half_send, half_recv, sum_send, sum_recv,
    part_send, part_recv, full_send, full_recv,
):
    nz = n_dp // 2
    n_plane = n_sec * n_mp
    n_tgt = n_dp // n_sec
    heads = wbuf.shape[0]
    nq = 4 if heads % 4 == 0 else 1
    hq = heads // nq
    half = nz * 32
    n_ids = ids_ref.shape[1]
    owner_rows = table_ref.shape[0]
    spans = q_ref.shape[0] // SPAN
    nbr = n_ids // spans
    out_rows = n_ids // n_plane
    k_long = nz // 2
    k_short = nz - 1 - k_long
    inv_root = 1.0 / math.sqrt(HEAD_DIM)

    me = lax.axis_index("dp")
    sec = lax.axis_index("section")
    mp = lax.axis_index("mp")
    z = me // 2
    core = lax.rem(me, 2)
    twin = 2 * z + (1 - core)
    here = sec * n_mp + mp
    asks = lax.rem(me, n_sec) == sec
    my_tgt = me // n_sec
    my_lane = lax.rem(me, n_sec)

    def up(step):
        return lax.rem(z + step + 2 * nz, nz)

    nexts = (2 * up(1) + core, 2 * up(-1) + core)

    def peer(j):
        p = lax.rem(here + j, n_plane)
        return (me, p // n_mp, lax.rem(p, n_mp))

    def remote(src, dst, send, recv, device):
        return pltpu.make_async_remote_copy(
            src_ref=src, dst_ref=dst, send_sem=send, recv_sem=recv,
            device_id=device, device_id_type=MESH,
        )

    def drain(ref, sem):
        pltpu.make_async_copy(ref, ref, sem).wait()

    barrier = pltpu.get_barrier_semaphore()

    def greet(device):
        pl.semaphore_signal(barrier, inc=1, device_id=device, device_id_type=MESH)

    greet((nexts[0], sec, mp))
    greet((nexts[1], sec, mp))
    greet((twin, sec, mp))

    @pl.loop(1, n_plane)
    def _(j):
        greet(peer(j))

    for k in range(n_tgt):
        other = sec + n_sec * k

        @pl.when(other != me)
        def _():
            greet((other, sec, mp))

        @pl.when(jnp.logical_or(other != me, my_lane != sec))
        def _():
            greet((other, my_lane, mp))

    expected = 3 + (n_plane - 1) + n_tgt
    expected = expected + jnp.where(asks, n_dp - 1 - 1, 0)
    pl.semaphore_wait(barrier, expected)

    def shard(src_z, parity, q):
        row = pl.multiple_of(parity * half + src_z * 32, 32)
        return wbuf.at[pl.ds(q * hq, hq), pl.ds(row, 32), :]

    def ring_copy(q, way, k, src_z):
        block = shard(src_z, core, q)
        return remote(block, block, ring_send, ring_recv.at[way, q, k], (nexts[way], sec, mp))

    def twin_copy(q, src_z):
        block = shard(src_z, core, q)
        return remote(block, block, twin_send, twin_recv.at[q], (twin, sec, mp))

    def last_step(q, way):
        return k_long if (q + way) % 2 == 0 else k_short

    own = pl.multiple_of(core * half + z * 32, 32)
    wbuf[:, pl.ds(own, 32), :] = w_ref[...]

    @pl.when(asks)
    def _():
        ids_buf[my_tgt] = ids_ref[...]

        @pl.loop(1, n_dp)
        def _(j):
            to = lax.rem(me + j, n_dp)
            remote(ids_ref, ids_buf.at[my_tgt], ids_send, ids_recv.at[my_tgt], (to, sec, mp)).start()

    for q in range(nq):
        for way in range(2):
            if last_step(q, way) > 0:
                ring_copy(q, way, 0, z).start()
        twin_copy(q, z).start()

    def gather_step(k, live, onward):
        for q in range(nq):
            for way in range(2):
                if not live(q, way):
                    continue
                src_z = up(-k) if way == 0 else up(k)
                ring_copy(q, way, k - 1, src_z).wait_recv()
                if onward(q, way):
                    ring_copy(q, way, k, src_z).start()
                twin_copy(q, src_z).start()

    def gather_steps(lo, hi):
        @pl.loop(lo, hi)
        def _(k):
            gather_step(k, lambda q, way: True, lambda q, way: True)

    def owner_of(ids):
        return ((ids.astype(F32) + 0.5) * (1.0 / owner_rows)).astype(jnp.int32)

    def base_of(ids):
        owner = owner_of(ids)
        dev = owner // n_mp
        slot = (lax.rem(dev, n_sec) * n_mp + lax.rem(owner, n_mp)) * (n_tgt * cap)
        return slot + (dev // n_sec) * cap

    ids = ids_ref[...]
    base_row = jnp.broadcast_to(base_of(ids).astype(F32), (n_ids, n_ids))
    row_no = iota((n_ids, n_ids), 0)
    col_no = iota((n_ids, n_ids), 1)
    base_col = jnp.sum(jnp.where(row_no == col_no, base_row, 0.0), axis=1, keepdims=True)
    same = jnp.logical_and(base_row == base_col, col_no < row_no)
    slot_col = jnp.sum(jnp.where(same, 1.0, 0.0), axis=1, keepdims=True)
    want = (base_col + slot_col).astype(jnp.int32)
    packed_rows = n_plane * n_tgt * cap
    place[...] = jnp.where(iota((n_ids, packed_rows), 1) == want, 1.0, 0.0).astype(BF16)

    wide = 2 * half
    enc_width = n_dp * e_rows
    pos = iota((wide, 1), 0)
    blk = pos // 32
    dev = 2 * lax.rem(blk, nz) + blk // nz
    inner = lax.rem(pos, 32)
    feature = jnp.where(inner < e_rows, dev * e_rows + inner, -1)
    pad_mat[...] = jnp.where(iota((wide, enc_width), 1) == feature, 1.0, 0.0).astype(BF16)

    first = max(1, min(2, k_short))
    second = max(first, min(4, k_short))
    gather_steps(1, first)

    for k in range(n_tgt):

        @pl.when(sec + n_sec * k != me)
        def _():
            drain(ids_buf.at[k], ids_recv.at[k])

    block_no = me * n_mp + mp
    upper = jnp.where(iota((n_ids, n_ids), 0) < iota((n_ids, n_ids), 1), 1.0, 0.0).astype(BF16)
    offs = jnp.concatenate(
        [jnp.broadcast_to(ids_buf[k], (PACK, n_ids)) for k in range(n_tgt)], axis=0
    ) - block_no * owner_rows
    mine = jnp.logical_and(offs >= 0, offs < owner_rows)
    slots = dot(jnp.where(mine, 1.0, 0.0).astype(BF16), upper)
    rank = lax.rem(iota((n_tgt * PACK, n_ids), 0), PACK).astype(F32)
    pick = jnp.logical_and(mine, slots == rank)
    wanted = jnp.sum(jnp.where(pick, offs.astype(F32) + 1.0, 0.0), axis=1, keepdims=True) - 1.0
    hot = jnp.where(
        iota((n_tgt * PACK, owner_rows), 1) == wanted.astype(jnp.int32), 1.0, 0.0
    ).astype(BF16)
    pack_buf[...] = dot(hot, table_ref[...]).astype(BF16).reshape(pack_buf.shape)

    for k in range(n_tgt):
        to = sec + n_sec * k
        away = jnp.logical_or(to != me, my_lane != sec)

        @pl.when(away)
        def _():
            remote(
                pack_buf.at[k], land_buf.at[my_tgt], pack_send.at[k], pack_recv.at[my_tgt],
                (to, my_lane, mp),
            ).start()

        @pl.when(jnp.logical_not(away))
        def _():
            land_buf[my_tgt] = pack_buf[k]

    gather_steps(first, second)

    for k in range(n_tgt):

        @pl.when(jnp.logical_or(sec + n_sec * k != me, my_lane != sec))
        def _():
            drain(land_buf.at[k], pack_recv.at[k])

    tight = n_tgt * cap
    row = iota((tight, n_tgt * PACK), 0)
    col = iota((tight, n_tgt * PACK), 1)
    squeeze = jnp.where((row // cap) * PACK + lax.rem(row, cap) == col, 1.0, 0.0).astype(BF16)
    landed = land_buf[...].reshape(n_tgt * PACK, enc_width)
    rows_buf[...] = dot(squeeze, landed).astype(BF16)
    spread[here] = rows_buf[...]

    @pl.loop(1, n_plane)
    def _(j):
        remote(rows_buf, spread.at[here], row_send, row_recv, peer(j)).start()

    gather_steps(second, k_short)
    if k_short >= 1:
        gather_step(k_short, lambda q, w: True, lambda q, w: last_step(q, w) > k_short)
    gather_step(k_long, lambda q, w: last_step(q, w) == k_long, lambda q, w: False)

    drain(spread.at[pl.ds(0, n_plane - 1)], row_recv)

    looked = dot(place[...], spread[...].reshape(packed_rows, enc_width))
    mean_square = jnp.mean(looked * looked, axis=-1, keepdims=True)
    encoded = (looked * lax.rsqrt(mean_square + 1e-06) * gain_ref[...]).astype(BF16)
    enc_buf[...] = dot(encoded, pad_mat[...], NT).astype(BF16)
    enct_buf[...] = dot(pad_mat[...], encoded, NT).astype(BF16)

    for q in range(nq):
        block = wbuf.at[pl.ds(q * hq, hq), pl.ds(pl.multiple_of((1 - core) * half, 32), half), :]
        drain(block, twin_recv.at[q])

    eacc[...] = jnp.zeros_like(eacc)

    @pl.loop(0, nq)
    def _(q):
        for hh in range(hq):
            h = q * hq + hh
            weight = wbuf[h]
            keyval = dot(enc_buf[...], weight).astype(BF16)
            lanes = pl.ds(pl.multiple_of(h * HEAD_DIM, HEAD_DIM), HEAD_DIM)
            for c in range(spans):
                keys = keyval[c * nbr:(c + 1) * nbr, :HEAD_DIM]
                values = keyval[c * nbr:(c + 1) * nbr, HEAD_DIM:]
                tokens = pl.ds(c * SPAN, SPAN)
                query = q_ref[tokens, lanes]
                grad = g_ref[tokens, lanes]
                scores = dot(query, keys, NT) * inv_root
                expo = jnp.exp(scores - jnp.max(scores, axis=-1, keepdims=True))
                prob = expo / jnp.sum(expo, axis=-1, keepdims=True)
                prob_b = prob.astype(BF16)
                attn_ref[tokens, lanes] = dot(prob_b, values).astype(BF16)
                grad_prob = dot(grad, values, NT)
                mixed = jnp.sum(grad_prob * prob, axis=-1, keepdims=True)
                grad_score = (prob * (grad_prob - mixed) * inv_root).astype(BF16)
                gq_ref[tokens, lanes] = dot(grad_score, keys).astype(BF16)
                rows = pl.ds(c * nbr, nbr)
                gbuf[h, rows, :HEAD_DIM] = dot(grad_score, query, TN).astype(BF16)
                gbuf[h, rows, HEAD_DIM:] = dot(prob_b, grad, TN).astype(BF16)
            eacc[...] += dot(gbuf[h], weight, NT)

    esend[...] = dot(eacc[...].astype(BF16), pad_mat[...]).astype(BF16)

    def out_slice(p):
        return pl.ds(pl.multiple_of(p * out_rows, out_rows), out_rows)

    eland[here] = esend[out_slice(here), :]

    @pl.loop(1, n_plane)
    def _(j):
        device = peer(j)
        p = device[1] * n_mp + device[2]
        remote(esend.at[out_slice(p), :], eland.at[here], part_send, part_recv, device).start()

    away_half = pl.ds(pl.multiple_of((1 - core) * half, 32), half)

    @pl.loop(0, heads)
    def _(h):
        pbuf[h] = dot(enct_buf[...], gbuf[h]).astype(BF16)
        remote(
            pbuf.at[h, away_half, :], sib.at[h], half_send, half_recv.at[h], (twin, sec, mp)
        ).start()

    def pair(q, dest_z):
        hs = pl.ds(q * hq, hq)
        a = pbuf[hs, pl.ds(pl.multiple_of(core * half + dest_z * 32, 32), 32), :]
        b = sib[hs, pl.ds(pl.multiple_of(dest_z * 32, 32), 32), :]
        return a.astype(F32) + b.astype(F32)

    def sum_copy(src, q, way, k):
        return remote(
            src, rbuf.at[way, k, pl.ds(q * hq, hq)], sum_send, sum_recv.at[way, q, k],
            (nexts[way], sec, mp),
        )

    def dest(way, steps):
        return up(steps) if way == 0 else up(-steps)

    for q in range(nq):
        for hh in range(hq):
            drain(sib.at[q * hq + hh], half_recv.at[q * hq + hh])
        for way in range(2):
            steps = last_step(q, way)
            if steps > 0:
                block = sbuf.at[way, pl.ds(q * hq, hq)]
                block[...] = pair(q, dest(way, steps)).astype(BF16)
                sum_copy(block, q, way, 0).start()

    def sum_step(k, live):
        for q in range(nq):
            for way in range(2):
                if not live(q, way):
                    continue
                block = rbuf.at[way, k - 1, pl.ds(q * hq, hq)]
                sum_copy(block, q, way, k - 1).wait_recv()
                total = block[...].astype(F32) + pair(q, dest(way, last_step(q, way) - k))
                block[...] = total.astype(BF16)
                sum_copy(block, q, way, k).start()

    middle = max(1, min(4, k_short))

    @pl.loop(1, middle)
    def _(k):
        sum_step(k, lambda q, w: True)

    drain(eland.at[pl.ds(0, n_plane - 1)], part_recv)
    mine_rows = jnp.sum(eland[...].astype(F32), axis=0).astype(BF16)
    gall[out_slice(here), :] = mine_rows

    @pl.loop(1, n_plane)
    def _(j):
        block = gall.at[out_slice(here), :]
        remote(block, block, full_send, full_recv, peer(j)).start()

    @pl.loop(middle, k_short)
    def _(k):
        sum_step(k, lambda q, w: True)

    if k_short >= 1:
        sum_step(k_short, lambda q, w: last_step(q, w) > k_short)

    for q in range(nq):
        total = pair(q, z)
        for way in range(2):
            steps = last_step(q, way)
            if steps > 0:
                block = rbuf.at[way, steps - 1, pl.ds(q * hq, hq)]
                sum_copy(block, q, way, steps - 1).wait_recv()
                total = total + block[...].astype(F32)
        wg_ref[pl.ds(q * hq, hq)] = total.astype(BF16)

    drain(gall.at[pl.ds(0, (n_plane - 1) * out_rows), :], full_recv)
    genc_ref[...] = gall[...]

    @pl.when(asks)
    def _():
        @pl.loop(1, n_dp)
        def _(j):
            drain(ids_ref, ids_send)

    for k in range(n_tgt):

        @pl.when(jnp.logical_or(sec + n_sec * k != me, my_lane != sec))
        def _():
            drain(pack_buf.at[k], pack_send.at[k])

    drain(spread.at[pl.ds(0, n_plane - 1)], row_send)
    sent = pl.ds(0, (nz - 1) * 32)
    drain(wbuf.at[:, sent, :], ring_send)
    drain(wbuf.at[:, pl.ds(0, half), :], twin_send)
    drain(sib, half_send)
    drain(sib.at[:, sent, :], sum_send)
    drain(eland.at[pl.ds(0, n_plane - 1)], part_send)
    drain(gall.at[pl.ds(0, (n_plane - 1) * out_rows), :], full_send)


def body(n_dp, n_sec, n_mp, neighbour_ids, embed_table, enc_gain, kv_weight, queries, grad_out):
    spans, nbr = neighbour_ids.shape
    n_ids = spans * nbr
    owner_rows, enc_width = embed_table.shape
    e_rows, local = kv_weight.shape[1], kv_weight.shape[3]
    heads = local // HEAD_DIM
    tokens = queries.shape[1]
    cap = 3 * n_ids // (2 * n_dp * n_mp)
    nz, n_plane, n_tgt = n_dp // 2, n_sec * n_mp, n_dp // n_sec
    half = nz * 32
    nq = 4 if heads % 4 == 0 else 1
    k_long = nz // 2
    weight = kv_weight[0].reshape(e_rows, 2, heads, HEAD_DIM).transpose(2, 0, 1, 3)
    weight = jnp.pad(weight.reshape(heads, e_rows, 2 * HEAD_DIM), ((0, 0), (0, 32 - e_rows), (0, 0)))
    vmem = pl.BlockSpec(memory_space=pltpu.VMEM)
    dma = pltpu.SemaphoreType.DMA
    out = pl.pallas_call(
        functools.partial(kernel, n_dp, n_sec, n_mp, cap, e_rows),
        out_shape=(
            jax.ShapeDtypeStruct((tokens, local), BF16),
            jax.ShapeDtypeStruct((tokens, local), BF16),
            jax.ShapeDtypeStruct((heads, 32, 2 * HEAD_DIM), BF16),
            jax.ShapeDtypeStruct((n_ids, enc_width), BF16),
        ),
        in_specs=[vmem] * 6,
        out_specs=(vmem,) * 4,
        scratch_shapes=[
            pltpu.VMEM((n_tgt, 1, n_ids), jnp.int32),
            pltpu.VMEM((n_tgt, PACK, enc_width), BF16),
            pltpu.VMEM((n_tgt, PACK, enc_width), BF16),
            pltpu.VMEM((n_tgt * cap, enc_width), BF16),
            pltpu.VMEM((n_plane, n_tgt * cap, enc_width), BF16),
            pltpu.VMEM((2 * half, enc_width), BF16),
            pltpu.VMEM((n_ids, n_plane * n_tgt * cap), BF16),
            pltpu.VMEM((n_ids, 2 * half), BF16),
            pltpu.VMEM((2 * half, n_ids), BF16),
            pltpu.VMEM((heads, 2 * half, 2 * HEAD_DIM), BF16),
            pltpu.VMEM((heads, n_ids, 2 * HEAD_DIM), BF16),
            pltpu.VMEM((n_ids, 2 * half), F32),
            pltpu.VMEM((heads, 2 * half, 2 * HEAD_DIM), BF16),
            pltpu.VMEM((heads, half, 2 * HEAD_DIM), BF16),
            pltpu.VMEM((2, heads, 32, 2 * HEAD_DIM), BF16),
            pltpu.VMEM((2, k_long, heads, 32, 2 * HEAD_DIM), BF16),
            pltpu.VMEM((n_ids, enc_width), BF16),
            pltpu.VMEM((n_plane, n_ids // n_plane, enc_width), BF16),
            pltpu.VMEM((n_ids, enc_width), BF16),
            dma, dma((n_tgt,)),
            dma((n_tgt,)), dma((n_tgt,)),
            dma, dma,
            dma, dma((2, nq, k_long)),
            dma, dma((nq,)),
            dma, dma((heads,)),
            dma, dma((2, nq, k_long)),
            dma, dma,
            dma, dma,
        ],
        compiler_params=pltpu.CompilerParams(
            collective_id=0, has_side_effects=True, vmem_limit_bytes=60 * 1024 * 1024
        ),
        name="layer",
    )(
        neighbour_ids.reshape(1, n_ids), embed_table, enc_gain.reshape(1, enc_width), weight,
        queries[0], grad_out[0],
    )
    attn, grad_query, weight_grad, grad_enc = out
    weight_grad = weight_grad[:, :e_rows].reshape(heads, e_rows, 2, HEAD_DIM).transpose(1, 2, 0, 3)
    return (
        attn[None],
        grad_query[None],
        weight_grad.reshape(1, e_rows, 2, local),
        grad_enc.reshape(spans, nbr, enc_width),
    )


def solution(mesh):
    in_specs = (
        P("dp", None),
        P(("dp", "mp"), None),
        P(),
        P("section", "dp", None, "mp"),
        P("section", "dp", "mp"),
        P("section", "dp", "mp"),
    )
    out_specs = (
        P("section", "dp", "mp"),
        P("section", "dp", "mp"),
        P("section", "dp", None, "mp"),
        P("dp", None, None),
    )
    sizes = (mesh.shape["dp"], mesh.shape["section"], mesh.shape["mp"])
    return jax.shard_map(
        functools.partial(body, *sizes), mesh=mesh, in_specs=in_specs, out_specs=out_specs,
        check_vma=False,
    )
```

time: 425 us -> 127 us (0.30)
  waiting for transfers between devices: 199 us -> 0 us
  blocking collectives: 117 us -> 0 us
  Pallas kernels: 0 us -> 114 us
  matrix products: 42.1 us -> 0 us
  local copies, waits for them, and re-layouts: 32.3 us -> 10.2 us
  between operations: 14.9 us -> 0.66 us
  other arithmetic: 11.3 us -> 0 us
  starting transfers between devices: 6.66 us -> 0 us
    pallas_call x0 -> x1, Pallas kernels: none -> 114 us  [body(): pl.pallas_call(functools.partial(kernel, n_dp, n_sec, n_mp, cap, e_rows),...]
    unnamed x3 -> x0, waiting for transfers between devices: 106 us -> none
    all_to_all x1 -> x0, waiting for transfers between devices: 93.3 us -> none  [encode_rows(): lax.all_to_all(found, ('dp', 'mp'), split_axis=0, concat_axis=0, tiled=True)]
    psum x1 -> x0, blocking collectives: 87 us -> none  [body(): summed = lax.psum(enc_term, ('section', 'mp')).astype(jnp.bfloat16)]
    dot_general x9 -> x0, matrix products: 42.1 us -> none  [the longest x1 8.91 us: body(): jnp.einsum('chqr,cqhd->crhd', grad_score, query_heads, preferred_element_...]
    all_to_all x1 -> x0, blocking collectives: 29.6 us -> none  [encode_rows(): lax.all_to_all(request, ('dp', 'mp'), split_axis=0, concat_axis=0, tiled=...]
    convert_element_type x4 -> x0, local copies, waits for them, and re-layouts: 8.44 us -> none  [the longest x1 5.58 us: body(): jnp.einsum('cre,crka->eka', encoded, grad_kv, preferred_element_type=jnp....]
    gather x3 -> x0, local copies, waits for them, and re-layouts: 6.97 us -> none  [the longest x2 4.23 us: encode_rows(): jnp.take(embed_table, lax.all_to_all(request, ('dp', 'mp'), split_axis=0,...]
  transfers between devices with their start and end apart: 3 -> 0, of which waited for: 2 -> 0; matrix products, arithmetic and copies ran while one was open for 11% -> 0% of each run, Pallas kernels for 0% -> 0%
where the time goes in v1:
time: 127 us; the launch traced here: 124 us
  Pallas kernels  114 us (90%)
  local copies, waits for them, and re-layouts  10.2 us (8%)
    pallas_call x1, Pallas kernels, body(): pl.pallas_call(functools.partial(kernel, n_dp, n_sec, n_mp, cap, e_rows),...  114 us
    unnamed x6, local copies, waits for them, and re-layouts  5.53 us

profile of v1, /device:TPU:6, one launch (start us, length us, event | category | flops | bytes accessed | tf_op | source)
XLA Modules:
  0.0 124.5 jit_solution(2346327240632059277)
XLA Ops:
  0.6 1.3 %copy.14 = s32[1,1,2,256]{3,1,2,0:T(1,128)} copy(s32[1,1,2,256]{3,2,1,0:T(2,128)} %bitcast.28) | data formatting | bytes 4096
  1.9 1.3 %reshape.27.gain_ref = f32[1,896]{1,0:T(1,128)} reshape(f32[896]{0:T(1024)} %param.8) | data formatting | bytes 7168 | tf_op jit(solution)/shard_map/reshape | solution.py:474
  3.2 1.0 reshape_squeeze.3
  4.2 0.7 pad.4.w_ref
  4.8 113.6 %layer.1 = (bf16[128,1024]{1,0:T(8,128)(2,1)}, bf16[128,1024]{1,0:T(8,128)(2,1)}, bf16[8,32,256]{2,1,0:T(8,128)(2,1)}, bf16[512,896]{1,0:T(8,128)(2,1)}) custom-call(s32[1,512]{1,0:T(1,128)} %bitcast.27, bf16[1000,896]{1,0:T(8,128)(2,1)} %table_ref.1, f32[1,896]{1,0:T(1,128)} %reshape.27.gain_ref, bf16[8,32,256]{2,1,0:T(8,128)(2,1)} %pad.4.w_ref, ...), custom_call_target="tpu_custom_call" | custom-call | tf_op jit(solution)/shard_map/layer/pallas_call | solution.py:429
  118.5 0.0 copy-start
  118.5 1.1 copy.16
  119.6 0.7 reshape.30
  120.2 1.7 %copy.20 = bf16[1,128,1024]{2,1,0:T(8,128)(2,1)} copy(bf16[1,128,1024]{2,1,0:T(8,128)(2,1)} %bitcast.25) | data formatting | bytes 524288
  121.9 1.7 %copy.21 = bf16[1,128,1024]{2,1,0:T(8,128)(2,1)} copy(bf16[1,128,1024]{2,1,0:T(8,128)(2,1)} %bitcast.24) | data formatting | bytes 524288
  123.6 0.0 copy-done
  123.6 0.9 copy.22
  (1 shorter events, 0.0 us)
Async XLA Ops:
  118.5 5.1 %copy-start = (bf16[512,896]{1,0:T(8,128)(2,1)S(1)}, bf16[512,896]{1,0:T(8,128)(2,1)}, u32[]{:S(2)}) copy-start(bf16[512,896]{1,0:T(8,128)(2,1)} %get-tuple-element.11) | copy-start | bytes 2752516

commit v2 on v1

--- a/solution.py
+++ b/solution.py
@@ -11,6 +11,7 @@
 HEAD_DIM = 128
 SPAN = 64
 PACK = 16
+HEAD_COLS = 2 * HEAD_DIM
 MESH = pl.DeviceIdType.MESH
 F32 = jnp.float32
 BF16 = jnp.bfloat16
@@ -31,7 +32,7 @@
     ids_ref, table_ref, gain_ref, w_ref, q_ref, g_ref,
     attn_ref, gq_ref, wg_ref, genc_ref,
     ids_buf, pack_buf, land_buf, rows_buf, spread, pad_mat, place,
-    enc_buf, enct_buf, wbuf, gbuf, eacc, pbuf, sib, sbuf, rbuf,
+    enc_buf, enct_buf, wbuf, gbuf, pbuf, sib, sbuf, rbuf,
     esend, eland, gall,
     ids_send, ids_recv, pack_send, pack_recv, row_send, row_recv,
     ring_send, ring_recv, twin_send, twin_recv,
@@ -41,17 +42,18 @@
     nz = n_dp // 2
     n_plane = n_sec * n_mp
     n_tgt = n_dp // n_sec
-    heads = wbuf.shape[0]
+    heads = wbuf.shape[1] // HEAD_COLS
     nq = 4 if heads % 4 == 0 else 1
     hq = heads // nq
+    cq = hq * HEAD_COLS
     half = nz * 32
-    n_ids = ids_ref.shape[1]
+    spans, nbr = ids_ref.shape
+    n_ids = spans * nbr
     owner_rows = table_ref.shape[0]
-    spans = q_ref.shape[0] // SPAN
-    nbr = n_ids // spans
-    out_rows = n_ids // n_plane
+    out_rows = nbr // n_plane
     k_long = nz // 2
     k_short = nz - 1 - k_long
+    group = 4 if heads % 4 == 0 else 1
     inv_root = 1.0 / math.sqrt(HEAD_DIM)
 
     me = lax.axis_index("dp")
@@ -113,7 +115,7 @@
 
     def shard(src_z, parity, q):
         row = pl.multiple_of(parity * half + src_z * 32, 32)
-        return wbuf.at[pl.ds(q * hq, hq), pl.ds(row, 32), :]
+        return wbuf.at[pl.ds(row, 32), pl.ds(q * cq, cq)]
 
     def ring_copy(q, way, k, src_z):
         block = shard(src_z, core, q)
@@ -127,7 +129,12 @@
         return k_long if (q + way) % 2 == 0 else k_short
 
     own = pl.multiple_of(core * half + z * 32, 32)
-    wbuf[:, pl.ds(own, 32), :] = w_ref[...]
+    wbuf[pl.ds(own, 32), :] = jnp.zeros((32, wbuf.shape[1]), BF16)
+    for part in range(2):
+        for h in range(heads):
+            wbuf[pl.ds(own, e_rows), pl.ds(h * HEAD_COLS + part * HEAD_DIM, HEAD_DIM)] = w_ref[
+                :, part, pl.ds(h * HEAD_DIM, HEAD_DIM)
+            ]
 
     @pl.when(asks)
     def _():
@@ -169,7 +176,7 @@
         slot = (lax.rem(dev, n_sec) * n_mp + lax.rem(owner, n_mp)) * (n_tgt * cap)
         return slot + (dev // n_sec) * cap
 
-    ids = ids_ref[...]
+    ids = jnp.concatenate([ids_ref[c:c + 1, :] for c in range(spans)], axis=1)
     base_row = jnp.broadcast_to(base_of(ids).astype(F32), (n_ids, n_ids))
     row_no = iota((n_ids, n_ids), 0)
     col_no = iota((n_ids, n_ids), 1)
@@ -202,7 +209,13 @@
     block_no = me * n_mp + mp
     upper = jnp.where(iota((n_ids, n_ids), 0) < iota((n_ids, n_ids), 1), 1.0, 0.0).astype(BF16)
     offs = jnp.concatenate(
-        [jnp.broadcast_to(ids_buf[k], (PACK, n_ids)) for k in range(n_tgt)], axis=0
+        [
+            jnp.concatenate(
+                [jnp.broadcast_to(ids_buf[k, c:c + 1, :], (PACK, nbr)) for c in range(spans)], axis=1
+            )
+            for k in range(n_tgt)
+        ],
+        axis=0,
     ) - block_no * owner_rows
     mine = jnp.logical_and(offs >= 0, offs < owner_rows)
     slots = dot(jnp.where(mine, 1.0, 0.0).astype(BF16), upper)
@@ -258,87 +271,115 @@
 
     looked = dot(place[...], spread[...].reshape(packed_rows, enc_width))
     mean_square = jnp.mean(looked * looked, axis=-1, keepdims=True)
-    encoded = (looked * lax.rsqrt(mean_square + 1e-06) * gain_ref[...]).astype(BF16)
+    encoded = (looked * lax.rsqrt(mean_square + 1e-06) * gain_ref[...][None, :]).astype(BF16)
     enc_buf[...] = dot(encoded, pad_mat[...], NT).astype(BF16)
     enct_buf[...] = dot(pad_mat[...], encoded, NT).astype(BF16)
 
     for q in range(nq):
-        block = wbuf.at[pl.ds(q * hq, hq), pl.ds(pl.multiple_of((1 - core) * half, 32), half), :]
-        drain(block, twin_recv.at[q])
-
-    eacc[...] = jnp.zeros_like(eacc)
-
-    @pl.loop(0, nq)
-    def _(q):
-        for hh in range(hq):
-            h = q * hq + hh
-            weight = wbuf[h]
-            keyval = dot(enc_buf[...], weight).astype(BF16)
-            lanes = pl.ds(pl.multiple_of(h * HEAD_DIM, HEAD_DIM), HEAD_DIM)
-            for c in range(spans):
-                keys = keyval[c * nbr:(c + 1) * nbr, :HEAD_DIM]
-                values = keyval[c * nbr:(c + 1) * nbr, HEAD_DIM:]
-                tokens = pl.ds(c * SPAN, SPAN)
-                query = q_ref[tokens, lanes]
-                grad = g_ref[tokens, lanes]
-                scores = dot(query, keys, NT) * inv_root
-                expo = jnp.exp(scores - jnp.max(scores, axis=-1, keepdims=True))
-                prob = expo / jnp.sum(expo, axis=-1, keepdims=True)
-                prob_b = prob.astype(BF16)
-                attn_ref[tokens, lanes] = dot(prob_b, values).astype(BF16)
-                grad_prob = dot(grad, values, NT)
-                mixed = jnp.sum(grad_prob * prob, axis=-1, keepdims=True)
-                grad_score = (prob * (grad_prob - mixed) * inv_root).astype(BF16)
-                gq_ref[tokens, lanes] = dot(grad_score, keys).astype(BF16)
-                rows = pl.ds(c * nbr, nbr)
-                gbuf[h, rows, :HEAD_DIM] = dot(grad_score, query, TN).astype(BF16)
-                gbuf[h, rows, HEAD_DIM:] = dot(prob_b, grad, TN).astype(BF16)
-            eacc[...] += dot(gbuf[h], weight, NT)
-
-    esend[...] = dot(eacc[...].astype(BF16), pad_mat[...]).astype(BF16)
-
-    def out_slice(p):
-        return pl.ds(pl.multiple_of(p * out_rows, out_rows), out_rows)
-
-    eland[here] = esend[out_slice(here), :]
-
-    @pl.loop(1, n_plane)
-    def _(j):
-        device = peer(j)
-        p = device[1] * n_mp + device[2]
-        remote(esend.at[out_slice(p), :], eland.at[here], part_send, part_recv, device).start()
+        other_half = pl.ds(pl.multiple_of((1 - core) * half, 32), half)
+        drain(wbuf.at[other_half, pl.ds(q * cq, cq)], twin_recv.at[q])
+
+    def attend(c):
+        tokens = pl.ds(c * SPAN, SPAN)
+        rows = pl.ds(c * nbr, nbr)
+
+        @pl.loop(0, heads // group)
+        def _(i):
+            start = pl.multiple_of(i * (group * HEAD_COLS), group * HEAD_COLS)
+            weight = wbuf[:, pl.ds(start, group * HEAD_COLS)]
+            keyval = dot(enc_buf[rows, :], weight).astype(BF16)
+            lane = pl.multiple_of(i * (group * HEAD_DIM), group * HEAD_DIM)
+            lanes = pl.ds(lane, group * HEAD_DIM)
+            query = q_ref[tokens, lanes]
+            grad = g_ref[tokens, lanes]
+
+            def cols(array, width, hh, part=0, size=HEAD_DIM):
+                return array[:, hh * width + part:hh * width + part + size]
+
+            each = range(group)
+            keys = [cols(keyval, HEAD_COLS, hh) for hh in each]
+            values = [cols(keyval, HEAD_COLS, hh, HEAD_DIM) for hh in each]
+            queries = [cols(query, HEAD_DIM, hh) for hh in each]
+            grads = [cols(grad, HEAD_DIM, hh) for hh in each]
+            scores = [dot(queries[hh], keys[hh], NT) * inv_root for hh in each]
+            grad_probs = [dot(grads[hh], values[hh], NT) for hh in each]
+            expos = [jnp.exp(x - jnp.max(x, axis=-1, keepdims=True)) for x in scores]
+            probs = [x / jnp.sum(x, axis=-1, keepdims=True) for x in expos]
+            probs_b = [x.astype(BF16) for x in probs]
+            mixed = [jnp.sum(a * b, axis=-1, keepdims=True) for a, b in zip(grad_probs, probs)]
+            grad_scores = [
+                (p * (g - m) * inv_root).astype(BF16) for p, g, m in zip(probs, grad_probs, mixed)
+            ]
+            attn = [dot(probs_b[hh], values[hh]).astype(BF16) for hh in each]
+            grad_q = [dot(grad_scores[hh], keys[hh]).astype(BF16) for hh in each]
+            attn_ref[tokens, lanes] = jnp.concatenate(attn, axis=1)
+            gq_ref[tokens, lanes] = jnp.concatenate(grad_q, axis=1)
+            grad_kv = []
+            for hh in each:
+                grad_kv.append(dot(grad_scores[hh], queries[hh], TN).astype(BF16))
+                grad_kv.append(dot(probs_b[hh], grads[hh], TN).astype(BF16))
+            gbuf[rows, pl.ds(start, group * HEAD_COLS)] = jnp.concatenate(grad_kv, axis=1)
+
+    def out_slice(c, p):
+        return pl.ds(pl.multiple_of(c * nbr + p * out_rows, out_rows), out_rows)
+
+    def send_parts(c):
+        rows = pl.ds(c * nbr, nbr)
+        term = dot(gbuf[rows, :], wbuf[...], NT).astype(BF16)
+        esend[rows, :] = dot(term, pad_mat[...]).astype(BF16)
+        eland[c, here] = esend[out_slice(c, here), :]
+
+        @pl.loop(1, n_plane)
+        def _(j):
+            device = peer(j)
+            p = device[1] * n_mp + device[2]
+            remote(
+                esend.at[out_slice(c, p), :], eland.at[c, here], part_send.at[c], part_recv.at[c],
+                device,
+            ).start()
+
+    def send_sums(c):
+        drain(eland.at[c, pl.ds(0, n_plane - 1)], part_recv.at[c])
+        mine_rows = jnp.sum(eland[c].astype(F32), axis=0).astype(BF16)
+        gall[out_slice(c, here), :] = mine_rows
+
+        @pl.loop(1, n_plane)
+        def _(j):
+            block = gall.at[out_slice(c, here), :]
+            remote(block, block, full_send.at[c], full_recv.at[c], peer(j)).start()
+
+    def columns(q):
+        return pl.ds(q * cq, cq)
 
     away_half = pl.ds(pl.multiple_of((1 - core) * half, 32), half)
 
-    @pl.loop(0, heads)
-    def _(h):
-        pbuf[h] = dot(enct_buf[...], gbuf[h]).astype(BF16)
+    def weight_grad(q):
+        pbuf[:, columns(q)] = dot(enct_buf[...], gbuf[:, columns(q)]).astype(BF16)
         remote(
-            pbuf.at[h, away_half, :], sib.at[h], half_send, half_recv.at[h], (twin, sec, mp)
+            pbuf.at[away_half, columns(q)], sib.at[:, columns(q)], half_send, half_recv.at[q],
+            (twin, sec, mp),
         ).start()
 
     def pair(q, dest_z):
-        hs = pl.ds(q * hq, hq)
-        a = pbuf[hs, pl.ds(pl.multiple_of(core * half + dest_z * 32, 32), 32), :]
-        b = sib[hs, pl.ds(pl.multiple_of(dest_z * 32, 32), 32), :]
+        a = pbuf[pl.ds(pl.multiple_of(core * half + dest_z * 32, 32), 32), columns(q)]
+        b = sib[pl.ds(pl.multiple_of(dest_z * 32, 32), 32), columns(q)]
         return a.astype(F32) + b.astype(F32)
 
     def sum_copy(src, q, way, k):
         return remote(
-            src, rbuf.at[way, k, pl.ds(q * hq, hq)], sum_send, sum_recv.at[way, q, k],
+            src, rbuf.at[way, k, :, columns(q)], sum_send, sum_recv.at[way, q, k],
             (nexts[way], sec, mp),
         )
 
     def dest(way, steps):
         return up(steps) if way == 0 else up(-steps)
 
-    for q in range(nq):
-        for hh in range(hq):
-            drain(sib.at[q * hq + hh], half_recv.at[q * hq + hh])
+    def sum_first(q):
+        drain(sib.at[:, columns(q)], half_recv.at[q])
         for way in range(2):
             steps = last_step(q, way)
             if steps > 0:
-                block = sbuf.at[way, pl.ds(q * hq, hq)]
+                block = sbuf.at[way, :, columns(q)]
                 block[...] = pair(q, dest(way, steps)).astype(BF16)
                 sum_copy(block, q, way, 0).start()
 
@@ -347,26 +388,35 @@
             for way in range(2):
                 if not live(q, way):
                     continue
-                block = rbuf.at[way, k - 1, pl.ds(q * hq, hq)]
+                block = rbuf.at[way, k - 1, :, columns(q)]
                 sum_copy(block, q, way, k - 1).wait_recv()
                 total = block[...].astype(F32) + pair(q, dest(way, last_step(q, way) - k))
                 block[...] = total.astype(BF16)
                 sum_copy(block, q, way, k).start()
 
+    for c in range(spans):
+        attend(c)
+        if c < spans - 1:
+            send_parts(c)
+    lag = 2 if nq > 2 else 0
+    for q in range(nq):
+        weight_grad(q)
+        if q == lag:
+            send_parts(spans - 1)
+        if q >= lag:
+            sum_first(q - lag)
+    for c in range(spans - 1):
+        send_sums(c)
+    for q in range(nq - lag, nq):
+        sum_first(q)
+
     middle = max(1, min(4, k_short))
 
     @pl.loop(1, middle)
     def _(k):
         sum_step(k, lambda q, w: True)
 
-    drain(eland.at[pl.ds(0, n_plane - 1)], part_recv)
-    mine_rows = jnp.sum(eland[...].astype(F32), axis=0).astype(BF16)
-    gall[out_slice(here), :] = mine_rows
-
-    @pl.loop(1, n_plane)
-    def _(j):
-        block = gall.at[out_slice(here), :]
-        remote(block, block, full_send, full_recv, peer(j)).start()
+    send_sums(spans - 1)
 
     @pl.loop(middle, k_short)
     def _(k):
@@ -380,12 +430,19 @@
         for way in range(2):
             steps = last_step(q, way)
             if steps > 0:
-                block = rbuf.at[way, steps - 1, pl.ds(q * hq, hq)]
+                block = rbuf.at[way, steps - 1, :, columns(q)]
                 sum_copy(block, q, way, steps - 1).wait_recv()
                 total = total + block[...].astype(F32)
-        wg_ref[pl.ds(q * hq, hq)] = total.astype(BF16)
-
-    drain(gall.at[pl.ds(0, (n_plane - 1) * out_rows), :], full_recv)
+        total = total.astype(BF16)
+        for hh in range(hq):
+            for part in range(2):
+                at = hh * HEAD_COLS + part * HEAD_DIM
+                wg_ref[:, part, pl.ds((q * hq + hh) * HEAD_DIM, HEAD_DIM)] = total[
+                    :e_rows, at:at + HEAD_DIM
+                ]
+
+    for c in range(spans):
+        drain(gall.at[pl.ds(0, (n_plane - 1) * out_rows), :], full_recv.at[c])
     genc_ref[...] = gall[...]
 
     @pl.when(asks)
@@ -402,12 +459,23 @@
 
     drain(spread.at[pl.ds(0, n_plane - 1)], row_send)
     sent = pl.ds(0, (nz - 1) * 32)
-    drain(wbuf.at[:, sent, :], ring_send)
-    drain(wbuf.at[:, pl.ds(0, half), :], twin_send)
+    drain(wbuf.at[sent, :], ring_send)
+    drain(wbuf.at[pl.ds(0, half), :], twin_send)
     drain(sib, half_send)
-    drain(sib.at[:, sent, :], sum_send)
-    drain(eland.at[pl.ds(0, n_plane - 1)], part_send)
-    drain(gall.at[pl.ds(0, (n_plane - 1) * out_rows), :], full_send)
+    drain(sib.at[sent, :], sum_send)
+    for c in range(spans):
+        drain(eland.at[c, pl.ds(0, n_plane - 1)], part_send.at[c])
+        drain(gall.at[pl.ds(0, (n_plane - 1) * out_rows), :], full_send.at[c])
+
+
+def settle(*refs):
+    count = len(refs) // 2
+    sems = refs[-1]
+    copies = [pltpu.make_async_copy(refs[i], refs[count + i], sems.at[i]) for i in range(count)]
+    for copy in copies:
+        copy.start()
+    for copy in copies:
+        copy.wait()
 
 
 def body(n_dp, n_sec, n_mp, neighbour_ids, embed_table, enc_gain, kv_weight, queries, grad_out):
@@ -422,8 +490,8 @@
     half = nz * 32
     nq = 4 if heads % 4 == 0 else 1
     k_long = nz // 2
-    weight = kv_weight[0].reshape(e_rows, 2, heads, HEAD_DIM).transpose(2, 0, 1, 3)
-    weight = jnp.pad(weight.reshape(heads, e_rows, 2 * HEAD_DIM), ((0, 0), (0, 32 - e_rows), (0, 0)))
+    cols = heads * HEAD_COLS
+    cols = heads * HEAD_COLS
     vmem = pl.BlockSpec(memory_space=pltpu.VMEM)
     dma = pltpu.SemaphoreType.DMA
     out = pl.pallas_call(
@@ -431,13 +499,13 @@
         out_shape=(
             jax.ShapeDtypeStruct((tokens, local), BF16),
             jax.ShapeDtypeStruct((tokens, local), BF16),
-            jax.ShapeDtypeStruct((heads, 32, 2 * HEAD_DIM), BF16),
+            jax.ShapeDtypeStruct((e_rows, 2, local), BF16),
             jax.ShapeDtypeStruct((n_ids, enc_width), BF16),
         ),
         in_specs=[vmem] * 6,
         out_specs=(vmem,) * 4,
         scratch_shapes=[
-            pltpu.VMEM((n_tgt, 1, n_ids), jnp.int32),
+            pltpu.VMEM((n_tgt, spans, nbr), jnp.int32),
             pltpu.VMEM((n_tgt, PACK, enc_width), BF16),
             pltpu.VMEM((n_tgt, PACK, enc_width), BF16),
             pltpu.VMEM((n_tgt * cap, enc_width), BF16),
@@ -446,40 +514,46 @@
             pltpu.VMEM((n_ids, n_plane * n_tgt * cap), BF16),
             pltpu.VMEM((n_ids, 2 * half), BF16),
             pltpu.VMEM((2 * half, n_ids), BF16),
-            pltpu.VMEM((heads, 2 * half, 2 * HEAD_DIM), BF16),
-            pltpu.VMEM((heads, n_ids, 2 * HEAD_DIM), BF16),
-            pltpu.VMEM((n_ids, 2 * half), F32),
-            pltpu.VMEM((heads, 2 * half, 2 * HEAD_DIM), BF16),
-            pltpu.VMEM((heads, half, 2 * HEAD_DIM), BF16),
-            pltpu.VMEM((2, heads, 32, 2 * HEAD_DIM), BF16),
-            pltpu.VMEM((2, k_long, heads, 32, 2 * HEAD_DIM), BF16),
+            pltpu.VMEM((2 * half, cols), BF16),
+            pltpu.VMEM((n_ids, cols), BF16),
+            pltpu.VMEM((2 * half, cols), BF16),
+            pltpu.VMEM((half, cols), BF16),
+            pltpu.VMEM((2, 32, cols), BF16),
+            pltpu.VMEM((2, k_long, 32, cols), BF16),
             pltpu.VMEM((n_ids, enc_width), BF16),
-            pltpu.VMEM((n_plane, n_ids // n_plane, enc_width), BF16),
+            pltpu.VMEM((spans, n_plane, nbr // n_plane, enc_width), BF16),
             pltpu.VMEM((n_ids, enc_width), BF16),
             dma, dma((n_tgt,)),
             dma((n_tgt,)), dma((n_tgt,)),
             dma, dma,
             dma, dma((2, nq, k_long)),
             dma, dma((nq,)),
-            dma, dma((heads,)),
+            dma, dma((nq,)),
             dma, dma((2, nq, k_long)),
-            dma, dma,
-            dma, dma,
+            dma((spans,)), dma((spans,)),
+            dma((spans,)), dma((spans,)),
         ],
         compiler_params=pltpu.CompilerParams(
             collective_id=0, has_side_effects=True, vmem_limit_bytes=60 * 1024 * 1024
         ),
         name="layer",
     )(
-        neighbour_ids.reshape(1, n_ids), embed_table, enc_gain.reshape(1, enc_width), weight,
+        neighbour_ids, embed_table, enc_gain, kv_weight[0],
         queries[0], grad_out[0],
     )
-    attn, grad_query, weight_grad, grad_enc = out
-    weight_grad = weight_grad[:, :e_rows].reshape(heads, e_rows, 2, HEAD_DIM).transpose(1, 2, 0, 3)
+    hbm = pl.BlockSpec(memory_space=pl.ANY)
+    attn, grad_query, weight_grad, grad_enc = pl.pallas_call(
+        settle,
+        out_shape=[jax.ShapeDtypeStruct(x.shape, x.dtype) for x in out],
+        in_specs=[hbm] * len(out),
+        out_specs=[hbm] * len(out),
+        scratch_shapes=[dma((len(out),))],
+        name="settle",
+    )(*out)
     return (
         attn[None],
         grad_query[None],
-        weight_grad.reshape(1, e_rows, 2, local),
+        weight_grad[None],
         grad_enc.reshape(spans, nbr, enc_width),
     )
 

time: 127 us -> 154 us (1.21)
  Pallas kernels: 114 us -> 152 us
  local copies, waits for them, and re-layouts: 10.2 us -> 0 us
    pallas_call x0 -> x1, Pallas kernels: none -> 48.3 us  [body(): pl.pallas_call(settle, out_shape=[jax.ShapeDtypeStruct(x.shape, x.dtype)...]
    pallas_call x1, Pallas kernels: 114 us -> 103 us  [body(): pl.pallas_call(functools.partial(kernel, n_dp, n_sec, n_mp, cap, e_rows),...]
    unnamed x6 -> x0, local copies, waits for them, and re-layouts: 5.53 us -> none
    reshape x3 -> x0, local copies, waits for them, and re-layouts: 1.97 us -> none  [the longest x1 1.27 us: body(): enc_gain.reshape(1, enc_width)]
where the time goes in v2:
time: 154 us; the launch traced here: 152 us
  Pallas kernels  152 us (99%)
    pallas_call x1, Pallas kernels, body(): pl.pallas_call(functools.partial(kernel, n_dp, n_sec, n_mp, cap, e_rows),...  103 us
    pallas_call x1, Pallas kernels, body(): pl.pallas_call(settle, out_shape=[jax.ShapeDtypeStruct(x.shape, x.dtype)...  48.3 us

profile of v2, /device:TPU:6, one launch (start us, length us, event | category | flops | bytes accessed | tf_op | source)
XLA Modules:
  0.0 152.5 jit_solution(18239632938260807805)
XLA Ops:
  0.6 103.4 %layer.1 = (bf16[128,1024]{1,0:T(8,128)(2,1)}, bf16[128,1024]{1,0:T(8,128)(2,1)}, bf16[28,2,1024]{2,1,0:T(2,128)(2,1)}, bf16[512,896]{1,0:T(8,128)(2,1)}) custom-call(s32[2,256]{1,0:T(2,128)} %ids_ref.1, bf16[1000,896]{1,0:T(8,128)(2,1)} %table_ref.1, f32[896]{0:T(1024)} %gain_ref.1, bf16[28,2,1024]{2,1,0:T(2,128)(2,1)} %bitcast.9, ...), custom_call_target="tpu_custom_call" | custom-call | tf_op jit(solution)/shard_map/layer/pallas_call | solution.py:497
  104.0 48.3 %settle.1 = (bf16[128,1024]{1,0:T(8,128)(2,1)}, bf16[128,1024]{1,0:T(8,128)(2,1)}, bf16[28,2,1024]{2,1,0:T(2,128)(2,1)}, bf16[512,896]{1,0:T(8,128)(2,1)}) custom-call(bf16[128,1024]{1,0:T(8,128)(2,1)} %get-tuple-element.12.refs_0_, bf16[128,1024]{1,0:T(8,128)(2,1)} %get-tuple-element.13.refs_1_, bf16[28,2,1024]{2,1,0:T(2,128)(2,1)} %get-tuple-element.14.refs_2_, ...), custom_call_target="tpu_custom_call" | custom-call | tf_op jit(solution)/shard_map/settle/pallas_call | solution.py:545

commit v3 on v2

--- a/solution.py
+++ b/solution.py
@@ -31,8 +31,8 @@
     n_dp, n_sec, n_mp, cap, e_rows,
     ids_ref, table_ref, gain_ref, w_ref, q_ref, g_ref,
     attn_ref, gq_ref, wg_ref, genc_ref,
-    ids_buf, pack_buf, land_buf, rows_buf, spread, pad_mat, place,
-    enc_buf, enct_buf, wbuf, gbuf, pbuf, sib, sbuf, rbuf,
+    ids_buf, pack_buf, land_buf, spread, pad_mat, place,
+    enc_buf, enct_buf, wbuf, gbuf, pbuf, sib, sbuf, rbuf, last_buf, last_out,
     esend, eland, gall,
     ids_send, ids_recv, pack_send, pack_recv, row_send, row_recv,
     ring_send, ring_recv, twin_send, twin_recv,
@@ -63,6 +63,9 @@
     core = lax.rem(me, 2)
     twin = 2 * z + (1 - core)
     here = sec * n_mp + mp
+    ny, nx = spread.shape[:2]
+    at_y = lax.rem(sec, ny)
+    at_x = (sec // ny) * n_mp + mp
     asks = lax.rem(me, n_sec) == sec
     my_tgt = me // n_sec
     my_lane = lax.rem(me, n_sec)
@@ -75,6 +78,13 @@
     def peer(j):
         p = lax.rem(here + j, n_plane)
         return (me, p // n_mp, lax.rem(p, n_mp))
+
+    def peer_x(j):
+        x = lax.rem(at_x + j, nx)
+        return (me, (x // n_mp) * ny + at_y, lax.rem(x, n_mp))
+
+    def peer_y(j):
+        return (me, (at_x // n_mp) * ny + lax.rem(at_y + j, ny), mp)
 
     def remote(src, dst, send, recv, device):
         return pltpu.make_async_remote_copy(
@@ -84,49 +94,6 @@
 
     def drain(ref, sem):
         pltpu.make_async_copy(ref, ref, sem).wait()
-
-    barrier = pltpu.get_barrier_semaphore()
-
-    def greet(device):
-        pl.semaphore_signal(barrier, inc=1, device_id=device, device_id_type=MESH)
-
-    greet((nexts[0], sec, mp))
-    greet((nexts[1], sec, mp))
-    greet((twin, sec, mp))
-
-    @pl.loop(1, n_plane)
-    def _(j):
-        greet(peer(j))
-
-    for k in range(n_tgt):
-        other = sec + n_sec * k
-
-        @pl.when(other != me)
-        def _():
-            greet((other, sec, mp))
-
-        @pl.when(jnp.logical_or(other != me, my_lane != sec))
-        def _():
-            greet((other, my_lane, mp))
-
-    expected = 3 + (n_plane - 1) + n_tgt
-    expected = expected + jnp.where(asks, n_dp - 1 - 1, 0)
-    pl.semaphore_wait(barrier, expected)
-
-    def shard(src_z, parity, q):
-        row = pl.multiple_of(parity * half + src_z * 32, 32)
-        return wbuf.at[pl.ds(row, 32), pl.ds(q * cq, cq)]
-
-    def ring_copy(q, way, k, src_z):
-        block = shard(src_z, core, q)
-        return remote(block, block, ring_send, ring_recv.at[way, q, k], (nexts[way], sec, mp))
-
-    def twin_copy(q, src_z):
-        block = shard(src_z, core, q)
-        return remote(block, block, twin_send, twin_recv.at[q], (twin, sec, mp))
-
-    def last_step(q, way):
-        return k_long if (q + way) % 2 == 0 else k_short
 
     own = pl.multiple_of(core * half + z * 32, 32)
     wbuf[pl.ds(own, 32), :] = jnp.zeros((32, wbuf.shape[1]), BF16)
@@ -135,6 +102,79 @@
             wbuf[pl.ds(own, e_rows), pl.ds(h * HEAD_COLS + part * HEAD_DIM, HEAD_DIM)] = w_ref[
                 :, part, pl.ds(h * HEAD_DIM, HEAD_DIM)
             ]
+
+    def owner_of(ids):
+        return ((ids.astype(F32) + 0.5) * (1.0 / owner_rows)).astype(jnp.int32)
+
+    def base_of(ids):
+        owner = owner_of(ids)
+        dev = owner // n_mp
+        dev_sec = lax.rem(dev, n_sec)
+        slot = lax.rem(dev_sec, ny) * nx + (dev_sec // ny) * n_mp + lax.rem(owner, n_mp)
+        return slot * (n_tgt * cap) + (dev // n_sec) * cap
+
+    ids = jnp.concatenate([ids_ref[c:c + 1, :] for c in range(spans)], axis=1)
+    base_row = jnp.broadcast_to(base_of(ids).astype(F32), (n_ids, n_ids))
+    row_no = iota((n_ids, n_ids), 0)
+    col_no = iota((n_ids, n_ids), 1)
+    base_col = jnp.sum(jnp.where(row_no == col_no, base_row, 0.0), axis=1, keepdims=True)
+    same = jnp.logical_and(base_row == base_col, col_no < row_no)
+    slot_col = jnp.sum(jnp.where(same, 1.0, 0.0), axis=1, keepdims=True)
+    want = (base_col + slot_col).astype(jnp.int32)
+    packed_rows = n_plane * n_tgt * cap
+    place[...] = jnp.where(iota((n_ids, packed_rows), 1) == want, 1.0, 0.0).astype(BF16)
+
+    wide = 2 * half
+    enc_width = n_dp * e_rows
+    pos = iota((wide, 1), 0)
+    blk = pos // 32
+    dev = 2 * lax.rem(blk, nz) + blk // nz
+    inner = lax.rem(pos, 32)
+    feature = jnp.where(inner < e_rows, dev * e_rows + inner, -1)
+    pad_mat[...] = jnp.where(iota((wide, enc_width), 1) == feature, 1.0, 0.0).astype(BF16)
+
+    barrier = pltpu.get_barrier_semaphore()
+
+    def greet(device):
+        pl.semaphore_signal(barrier, inc=1, device_id=device, device_id_type=MESH)
+
+    greet((nexts[0], sec, mp))
+    greet((nexts[1], sec, mp))
+    greet((twin, sec, mp))
+
+    @pl.loop(1, n_plane)
+    def _(j):
+        greet(peer(j))
+
+    for k in range(n_tgt):
+        other = sec + n_sec * k
+
+        @pl.when(other != me)
+        def _():
+            greet((other, sec, mp))
+
+        @pl.when(jnp.logical_or(other != me, my_lane != sec))
+        def _():
+            greet((other, my_lane, mp))
+
+    expected = 3 + (n_plane - 1) + n_tgt
+    expected = expected + jnp.where(asks, n_dp - 1 - 1, 0)
+    pl.semaphore_wait(barrier, expected)
+
+    def shard(src_z, parity, q):
+        row = pl.multiple_of(parity * half + src_z * 32, 32)
+        return wbuf.at[pl.ds(row, 32), pl.ds(q * cq, cq)]
+
+    def ring_copy(q, way, k, src_z):
+        block = shard(src_z, core, q)
+        return remote(block, block, ring_send, ring_recv.at[way, q, k], (nexts[way], sec, mp))
+
+    def twin_copy(q, src_z):
+        block = shard(src_z, core, q)
+        return remote(block, block, twin_send, twin_recv.at[q], (twin, sec, mp))
+
+    def last_step(q, way):
+        return k_long if (q + way) % 2 == 0 else k_short
 
     @pl.when(asks)
     def _():
@@ -166,35 +206,6 @@
         @pl.loop(lo, hi)
         def _(k):
             gather_step(k, lambda q, way: True, lambda q, way: True)
-
-    def owner_of(ids):
-        return ((ids.astype(F32) + 0.5) * (1.0 / owner_rows)).astype(jnp.int32)
-
-    def base_of(ids):
-        owner = owner_of(ids)
-        dev = owner // n_mp
-        slot = (lax.rem(dev, n_sec) * n_mp + lax.rem(owner, n_mp)) * (n_tgt * cap)
-        return slot + (dev // n_sec) * cap
-
-    ids = jnp.concatenate([ids_ref[c:c + 1, :] for c in range(spans)], axis=1)
-    base_row = jnp.broadcast_to(base_of(ids).astype(F32), (n_ids, n_ids))
-    row_no = iota((n_ids, n_ids), 0)
-    col_no = iota((n_ids, n_ids), 1)
-    base_col = jnp.sum(jnp.where(row_no == col_no, base_row, 0.0), axis=1, keepdims=True)
-    same = jnp.logical_and(base_row == base_col, col_no < row_no)
-    slot_col = jnp.sum(jnp.where(same, 1.0, 0.0), axis=1, keepdims=True)
-    want = (base_col + slot_col).astype(jnp.int32)
-    packed_rows = n_plane * n_tgt * cap
-    place[...] = jnp.where(iota((n_ids, packed_rows), 1) == want, 1.0, 0.0).astype(BF16)
-
-    wide = 2 * half
-    enc_width = n_dp * e_rows
-    pos = iota((wide, 1), 0)
-    blk = pos // 32
-    dev = 2 * lax.rem(blk, nz) + blk // nz
-    inner = lax.rem(pos, 32)
-    feature = jnp.where(inner < e_rows, dev * e_rows + inner, -1)
-    pad_mat[...] = jnp.where(iota((wide, enc_width), 1) == feature, 1.0, 0.0).astype(BF16)
 
     first = max(1, min(2, k_short))
     second = max(first, min(4, k_short))
@@ -255,19 +266,45 @@
     col = iota((tight, n_tgt * PACK), 1)
     squeeze = jnp.where((row // cap) * PACK + lax.rem(row, cap) == col, 1.0, 0.0).astype(BF16)
     landed = land_buf[...].reshape(n_tgt * PACK, enc_width)
-    rows_buf[...] = dot(squeeze, landed).astype(BF16)
-    spread[here] = rows_buf[...]
-
-    @pl.loop(1, n_plane)
-    def _(j):
-        remote(rows_buf, spread.at[here], row_send, row_recv, peer(j)).start()
-
-    gather_steps(second, k_short)
+    spread[at_y, at_x] = dot(squeeze, landed).astype(BF16)
+
+    cut = 128 * ((enc_width // 128 + 1) // 2)
+    lanes_a, lanes_b = pl.ds(0, cut), pl.ds(cut, enc_width - cut)
+
+    def spread_along(count, peer_of, block, stage):
+        if count > 1:
+
+            @pl.loop(1, count)
+            def _(j):
+                remote(block, block, row_send.at[stage], row_recv.at[stage], peer_of(j)).start()
+
+    row_stages = (
+        spread.at[0, pl.ds(0, nx - 1), :, lanes_a] if nx > 1 else None,
+        spread.at[pl.ds(0, ny - 1), :, :, lanes_a] if ny > 1 else None,
+        spread.at[pl.ds(0, ny - 1), 0, :, lanes_b] if ny > 1 else None,
+        spread.at[:, pl.ds(0, nx - 1), :, lanes_b] if nx > 1 else None,
+    )
+
+    def row_drain(stage, sems):
+        if row_stages[stage] is not None:
+            drain(row_stages[stage], sems.at[stage])
+
+    spread_along(nx, peer_x, spread.at[at_y, at_x, :, lanes_a], 0)
+    spread_along(ny, peer_y, spread.at[at_y, at_x, :, lanes_b], 2)
+    third = max(second, min(5, k_short))
+    gather_steps(second, third)
+    row_drain(0, row_recv)
+    spread_along(ny, peer_y, spread.at[at_y, :, :, lanes_a], 1)
+    row_drain(2, row_recv)
+    spread_along(nx, peer_x, spread.at[:, at_x, :, lanes_b], 3)
+
+    gather_steps(third, k_short)
     if k_short >= 1:
         gather_step(k_short, lambda q, w: True, lambda q, w: last_step(q, w) > k_short)
     gather_step(k_long, lambda q, w: last_step(q, w) == k_long, lambda q, w: False)
 
-    drain(spread.at[pl.ds(0, n_plane - 1)], row_recv)
+    row_drain(1, row_recv)
+    row_drain(3, row_recv)
 
     looked = dot(place[...], spread[...].reshape(packed_rows, enc_width))
     mean_square = jnp.mean(looked * looked, axis=-1, keepdims=True)
@@ -279,46 +316,42 @@
         other_half = pl.ds(pl.multiple_of((1 - core) * half, 32), half)
         drain(wbuf.at[other_half, pl.ds(q * cq, cq)], twin_recv.at[q])
 
-    def attend(c):
+    def attend(c, i):
         tokens = pl.ds(c * SPAN, SPAN)
         rows = pl.ds(c * nbr, nbr)
-
-        @pl.loop(0, heads // group)
-        def _(i):
-            start = pl.multiple_of(i * (group * HEAD_COLS), group * HEAD_COLS)
-            weight = wbuf[:, pl.ds(start, group * HEAD_COLS)]
-            keyval = dot(enc_buf[rows, :], weight).astype(BF16)
-            lane = pl.multiple_of(i * (group * HEAD_DIM), group * HEAD_DIM)
-            lanes = pl.ds(lane, group * HEAD_DIM)
-            query = q_ref[tokens, lanes]
-            grad = g_ref[tokens, lanes]
-
-            def cols(array, width, hh, part=0, size=HEAD_DIM):
-                return array[:, hh * width + part:hh * width + part + size]
-
-            each = range(group)
-            keys = [cols(keyval, HEAD_COLS, hh) for hh in each]
-            values = [cols(keyval, HEAD_COLS, hh, HEAD_DIM) for hh in each]
-            queries = [cols(query, HEAD_DIM, hh) for hh in each]
-            grads = [cols(grad, HEAD_DIM, hh) for hh in each]
-            scores = [dot(queries[hh], keys[hh], NT) * inv_root for hh in each]
-            grad_probs = [dot(grads[hh], values[hh], NT) for hh in each]
-            expos = [jnp.exp(x - jnp.max(x, axis=-1, keepdims=True)) for x in scores]
-            probs = [x / jnp.sum(x, axis=-1, keepdims=True) for x in expos]
-            probs_b = [x.astype(BF16) for x in probs]
-            mixed = [jnp.sum(a * b, axis=-1, keepdims=True) for a, b in zip(grad_probs, probs)]
-            grad_scores = [
-                (p * (g - m) * inv_root).astype(BF16) for p, g, m in zip(probs, grad_probs, mixed)
-            ]
-            attn = [dot(probs_b[hh], values[hh]).astype(BF16) for hh in each]
-            grad_q = [dot(grad_scores[hh], keys[hh]).astype(BF16) for hh in each]
-            attn_ref[tokens, lanes] = jnp.concatenate(attn, axis=1)
-            gq_ref[tokens, lanes] = jnp.concatenate(grad_q, axis=1)
-            grad_kv = []
-            for hh in each:
-                grad_kv.append(dot(grad_scores[hh], queries[hh], TN).astype(BF16))
-                grad_kv.append(dot(probs_b[hh], grads[hh], TN).astype(BF16))
-            gbuf[rows, pl.ds(start, group * HEAD_COLS)] = jnp.concatenate(grad_kv, axis=1)
+        start = i * (group * HEAD_COLS)
+        weight = wbuf[:, pl.ds(start, group * HEAD_COLS)]
+        keyval = dot(enc_buf[rows, :], weight).astype(BF16)
+        lanes = pl.ds(i * (group * HEAD_DIM), group * HEAD_DIM)
+        query = q_ref[tokens, lanes]
+        grad = g_ref[tokens, lanes]
+
+        def cols(array, width, hh, part=0, size=HEAD_DIM):
+            return array[:, hh * width + part:hh * width + part + size]
+
+        each = range(group)
+        keys = [cols(keyval, HEAD_COLS, hh) for hh in each]
+        values = [cols(keyval, HEAD_COLS, hh, HEAD_DIM) for hh in each]
+        queries = [cols(query, HEAD_DIM, hh) for hh in each]
+        grads = [cols(grad, HEAD_DIM, hh) for hh in each]
+        scores = [dot(queries[hh], keys[hh], NT) * inv_root for hh in each]
+        grad_probs = [dot(grads[hh], values[hh], NT) for hh in each]
+        expos = [jnp.exp(x - jnp.max(x, axis=-1, keepdims=True)) for x in scores]
+        probs = [x / jnp.sum(x, axis=-1, keepdims=True) for x in expos]
+        probs_b = [x.astype(BF16) for x in probs]
+        mixed = [jnp.sum(a * b, axis=-1, keepdims=True) for a, b in zip(grad_probs, probs)]
+        grad_scores = [
+            (p * (g - m) * inv_root).astype(BF16) for p, g, m in zip(probs, grad_probs, mixed)
+        ]
+        attn = [dot(probs_b[hh], values[hh]).astype(BF16) for hh in each]
+        grad_q = [dot(grad_scores[hh], keys[hh]).astype(BF16) for hh in each]
+        attn_ref[tokens, lanes] = jnp.concatenate(attn, axis=1)
+        gq_ref[tokens, lanes] = jnp.concatenate(grad_q, axis=1)
+        grad_kv = []
+        for hh in each:
+            grad_kv.append(dot(grad_scores[hh], queries[hh], TN).astype(BF16))
+            grad_kv.append(dot(probs_b[hh], grads[hh], TN).astype(BF16))
+        gbuf[rows, pl.ds(start, group * HEAD_COLS)] = jnp.concatenate(grad_kv, axis=1)
 
     def out_slice(c, p):
         return pl.ds(pl.multiple_of(c * nbr + p * out_rows, out_rows), out_rows)
@@ -365,10 +398,18 @@
         b = sib[pl.ds(pl.multiple_of(dest_z * 32, 32), 32), columns(q)]
         return a.astype(F32) + b.astype(F32)
 
+    def narrow(q, way, k):
+        return k < last_step(q, way) - 2
+
+    def slot_of(q, way, k):
+        if narrow(q, way, k):
+            return rbuf.at[way, k, :, columns(q)]
+        return last_buf.at[2 * way + k - last_step(q, way) + 2, :, columns(q)]
+
     def sum_copy(src, q, way, k):
+        sem = sum_send.at[0 if narrow(q, way, k) else 1]
         return remote(
-            src, rbuf.at[way, k, :, columns(q)], sum_send, sum_recv.at[way, q, k],
-            (nexts[way], sec, mp),
+            src, slot_of(q, way, k), sem, sum_recv.at[way, q, k], (nexts[way], sec, mp)
         )
 
     def dest(way, steps):
@@ -379,60 +420,68 @@
         for way in range(2):
             steps = last_step(q, way)
             if steps > 0:
-                block = sbuf.at[way, :, columns(q)]
-                block[...] = pair(q, dest(way, steps)).astype(BF16)
+                block = (sbuf if narrow(q, way, 0) else last_out).at[way, :, columns(q)]
+                block[...] = pair(q, dest(way, steps)).astype(block.dtype)
                 sum_copy(block, q, way, 0).start()
 
-    def sum_step(k, live):
-        for q in range(nq):
+    def sum_step(qs, k):
+        for q in qs:
             for way in range(2):
-                if not live(q, way):
+                steps = last_step(q, way)
+                if not 1 <= k < steps:
                     continue
-                block = rbuf.at[way, k - 1, :, columns(q)]
+                block = slot_of(q, way, k - 1)
                 sum_copy(block, q, way, k - 1).wait_recv()
-                total = block[...].astype(F32) + pair(q, dest(way, last_step(q, way) - k))
-                block[...] = total.astype(BF16)
+                total = block[...].astype(F32) + pair(q, dest(way, steps - k))
+                if narrow(q, way, k - 1) and not narrow(q, way, k):
+                    block = last_out.at[way, :, columns(q)]
+                block[...] = total.astype(block.dtype)
                 sum_copy(block, q, way, k).start()
 
+    groups = heads // group
+    per = nq // groups
+    quarters = [range(i * per, (i + 1) * per) for i in range(groups)]
+
+    for i in range(groups - 1):
+        for c in range(spans):
+            attend(c, i)
+        for q in quarters[i]:
+            weight_grad(q)
+    ahead = 0
     for c in range(spans):
-        attend(c)
-        if c < spans - 1:
-            send_parts(c)
-    lag = 2 if nq > 2 else 0
-    for q in range(nq):
+        attend(c, groups - 1)
+        for i in range(groups - 1):
+            if c == 0:
+                for q in quarters[i]:
+                    sum_first(q)
+            else:
+                sum_step(quarters[i], c)
+                ahead = c
+    for q in quarters[-1]:
         weight_grad(q)
-        if q == lag:
-            send_parts(spans - 1)
-        if q >= lag:
-            sum_first(q - lag)
-    for c in range(spans - 1):
-        send_sums(c)
-    for q in range(nq - lag, nq):
+    send_parts(0)
+    ahead += 1
+    for i in range(groups - 1):
+        sum_step(quarters[i], ahead)
+    for q in quarters[-1]:
         sum_first(q)
-
-    middle = max(1, min(4, k_short))
-
-    @pl.loop(1, middle)
-    def _(k):
-        sum_step(k, lambda q, w: True)
-
-    send_sums(spans - 1)
-
-    @pl.loop(middle, k_short)
-    def _(k):
-        sum_step(k, lambda q, w: True)
-
-    if k_short >= 1:
-        sum_step(k_short, lambda q, w: last_step(q, w) > k_short)
+    for c in range(1, spans):
+        send_parts(c)
+    for k in range(1, k_long + 1):
+        for i in range(groups - 1):
+            sum_step(quarters[i], ahead + k)
+        sum_step(quarters[-1], k)
+        if k == min(4, k_long):
+            for c in range(spans):
+                send_sums(c)
 
     for q in range(nq):
         total = pair(q, z)
         for way in range(2):
             steps = last_step(q, way)
             if steps > 0:
-                block = rbuf.at[way, steps - 1, :, columns(q)]
-                sum_copy(block, q, way, steps - 1).wait_recv()
-                total = total + block[...].astype(F32)
+                sum_copy(slot_of(q, way, steps - 1), q, way, steps - 1).wait_recv()
+                total = total + slot_of(q, way, steps - 1)[...]
         total = total.astype(BF16)
         for hh in range(hq):
             for part in range(2):
@@ -457,12 +506,17 @@
         def _():
             drain(pack_buf.at[k], pack_send.at[k])
 
-    drain(spread.at[pl.ds(0, n_plane - 1)], row_send)
+    for stage in range(4):
+        row_drain(stage, row_send)
     sent = pl.ds(0, (nz - 1) * 32)
     drain(wbuf.at[sent, :], ring_send)
     drain(wbuf.at[pl.ds(0, half), :], twin_send)
     drain(sib, half_send)
-    drain(sib.at[sent, :], sum_send)
+    if k_long > 2:
+        narrow_sent = pl.ds(0, (k_long - 2 + max(0, k_short - 2)) * 32)
+        drain(sib.at[narrow_sent, :], sum_send.at[0])
+    last_two = min(2, k_long) + min(2, k_short)
+    drain(last_buf.at[pl.ds(0, last_two)], sum_send.at[1])
     for c in range(spans):
         drain(eland.at[c, pl.ds(0, n_plane - 1)], part_send.at[c])
         drain(gall.at[pl.ds(0, (n_plane - 1) * out_rows), :], full_send.at[c])
@@ -487,6 +541,7 @@
     tokens = queries.shape[1]
     cap = 3 * n_ids // (2 * n_dp * n_mp)
     nz, n_plane, n_tgt = n_dp // 2, n_sec * n_mp, n_dp // n_sec
+    ny = max(1, n_sec // 2)
     half = nz * 32
     nq = 4 if heads % 4 == 0 else 1
     k_long = nz // 2
@@ -508,8 +563,7 @@
             pltpu.VMEM((n_tgt, spans, nbr), jnp.int32),
             pltpu.VMEM((n_tgt, PACK, enc_width), BF16),
             pltpu.VMEM((n_tgt, PACK, enc_width), BF16),
-            pltpu.VMEM((n_tgt * cap, enc_width), BF16),
-            pltpu.VMEM((n_plane, n_tgt * cap, enc_width), BF16),
+            pltpu.VMEM((ny, n_plane // ny, n_tgt * cap, enc_width), BF16),
             pltpu.VMEM((2 * half, enc_width), BF16),
             pltpu.VMEM((n_ids, n_plane * n_tgt * cap), BF16),
             pltpu.VMEM((n_ids, 2 * half), BF16),
@@ -520,16 +574,18 @@
             pltpu.VMEM((half, cols), BF16),
             pltpu.VMEM((2, 32, cols), BF16),
             pltpu.VMEM((2, k_long, 32, cols), BF16),
+            pltpu.VMEM((4, 32, cols), F32),
+            pltpu.VMEM((2, 32, cols), F32),
             pltpu.VMEM((n_ids, enc_width), BF16),
             pltpu.VMEM((spans, n_plane, nbr // n_plane, enc_width), BF16),
             pltpu.VMEM((n_ids, enc_width), BF16),
             dma, dma((n_tgt,)),
             dma((n_tgt,)), dma((n_tgt,)),
-            dma, dma,
+            dma((4,)), dma((4,)),
             dma, dma((2, nq, k_long)),
             dma, dma((nq,)),
             dma, dma((nq,)),
-            dma, dma((2, nq, k_long)),
+            dma((2,)), dma((2, nq, k_long)),
             dma((spans,)), dma((spans,)),
             dma((spans,)), dma((spans,)),
         ],
@@ -545,7 +601,7 @@
     attn, grad_query, weight_grad, grad_enc = pl.pallas_call(
         settle,
         out_shape=[jax.ShapeDtypeStruct(x.shape, x.dtype) for x in out],
-        in_specs=[hbm] * len(out),
+        in_specs=[vmem] * len(out),
         out_specs=[hbm] * len(out),
         scratch_shapes=[dma((len(out),))],
         name="settle",

time: 154 us -> 113 us (0.73); the launches traced: 152 us -> 113 us
  Pallas kernels: 152 us -> 112 us
    pallas_call x1, Pallas kernels: 48.3 us -> 2.55 us  [body(): pl.pallas_call(settle, out_shape=[jax.ShapeDtypeStruct(x.shape, x.dtype)...]
    pallas_call x1, Pallas kernels: 103 us -> 110 us  [body(): pl.pallas_call(functools.partial(kernel, n_dp, n_sec, n_mp, cap, e_rows),...]
where the time goes in v3:
time: 113 us
  Pallas kernels  112 us (99%)
    pallas_call x1, Pallas kernels, body(): pl.pallas_call(functools.partial(kernel, n_dp, n_sec, n_mp, cap, e_rows),...  110 us
    pallas_call x1, Pallas kernels, body(): pl.pallas_call(settle, out_shape=[jax.ShapeDtypeStruct(x.shape, x.dtype)...  2.55 us

profile of v3, /device:TPU:6, one launch (start us, length us, event | category | flops | bytes accessed | tf_op | source)
XLA Modules:
  0.0 113.0 jit_solution(11348154484499850558)
XLA Ops:
  0.6 109.7 %layer.1 = (bf16[128,1024]{1,0:T(8,128)(2,1)}, bf16[128,1024]{1,0:T(8,128)(2,1)}, bf16[28,2,1024]{2,1,0:T(2,128)(2,1)}, bf16[512,896]{1,0:T(8,128)(2,1)}) custom-call(s32[2,256]{1,0:T(2,128)} %ids_ref.1, bf16[1000,896]{1,0:T(8,128)(2,1)} %table_ref.1, f32[896]{0:T(1024)} %gain_ref.1, bf16[28,2,1024]{2,1,0:T(2,128)(2,1)} %bitcast.9, ...), custom_call_target="tpu_custom_call" | custom-call | tf_op jit(solution)/shard_map/layer/pallas_call | solution.py:552
  110.3 2.5 %settle.1 = (bf16[128,1024]{1,0:T(8,128)(2,1)}, bf16[128,1024]{1,0:T(8,128)(2,1)}, bf16[28,2,1024]{2,1,0:T(2,128)(2,1)}, bf16[512,896]{1,0:T(8,128)(2,1)}) custom-call(bf16[128,1024]{1,0:T(8,128)(2,1)} %get-tuple-element.12.refs_0_, bf16[128,1024]{1,0:T(8,128)(2,1)} %get-tuple-element.13.refs_1_, bf16[28,2,1024]{2,1,0:T(2,128)(2,1)} %get-tuple-element.14.refs_2_, ...), custom_call_target="tpu_custom_call" | custom-call | tf_op jit(solution)/shard_map/settle/pallas_call | solution.py:601

commit v4 on v3

--- a/solution.py
+++ b/solution.py
@@ -142,9 +142,13 @@
     greet((nexts[1], sec, mp))
     greet((twin, sec, mp))
 
-    @pl.loop(1, n_plane)
+    @pl.loop(1, nx)
     def _(j):
-        greet(peer(j))
+        greet(peer_x(j))
+
+    @pl.loop(1, ny)
+    def _(j):
+        greet(peer_y(j))
 
     for k in range(n_tgt):
         other = sec + n_sec * k
@@ -157,7 +161,7 @@
         def _():
             greet((other, my_lane, mp))
 
-    expected = 3 + (n_plane - 1) + n_tgt
+    expected = 3 + (nx - 1) + (ny - 1) + n_tgt
     expected = expected + jnp.where(asks, n_dp - 1 - 1, 0)
     pl.semaphore_wait(barrier, expected)
 
@@ -459,13 +463,12 @@
                 ahead = c
     for q in quarters[-1]:
         weight_grad(q)
-    send_parts(0)
     ahead += 1
     for i in range(groups - 1):
         sum_step(quarters[i], ahead)
     for q in quarters[-1]:
         sum_first(q)
-    for c in range(1, spans):
+    for c in range(spans):
         send_parts(c)
     for k in range(1, k_long + 1):
         for i in range(groups - 1):

time: 113 us -> 114 us (level)
  no operation moved by 1% of the time
where the time goes in v4:
time: 114 us
  Pallas kernels  113 us (99%)
    pallas_call x1, Pallas kernels, body(): pl.pallas_call(functools.partial(kernel, n_dp, n_sec, n_mp, cap, e_rows),...  110 us
    pallas_call x1, Pallas kernels, body(): pl.pallas_call(settle, out_shape=[jax.ShapeDtypeStruct(x.shape, x.dtype)...  2.55 us

profile of v4, /device:TPU:6, one launch (start us, length us, event | category | flops | bytes accessed | tf_op | source)
XLA Modules:
  0.0 113.7 jit_solution(1268226152075634479)
XLA Ops:
  0.6 110.3 %layer.1 = (bf16[128,1024]{1,0:T(8,128)(2,1)}, bf16[128,1024]{1,0:T(8,128)(2,1)}, bf16[28,2,1024]{2,1,0:T(2,128)(2,1)}, bf16[512,896]{1,0:T(8,128)(2,1)}) custom-call(s32[2,256]{1,0:T(2,128)} %ids_ref.1, bf16[1000,896]{1,0:T(8,128)(2,1)} %table_ref.1, f32[896]{0:T(1024)} %gain_ref.1, bf16[28,2,1024]{2,1,0:T(2,128)(2,1)} %bitcast.9, ...), custom_call_target="tpu_custom_call" | custom-call | tf_op jit(solution)/shard_map/layer/pallas_call | solution.py:555
  111.0 2.5 %settle.1 = (bf16[128,1024]{1,0:T(8,128)(2,1)}, bf16[128,1024]{1,0:T(8,128)(2,1)}, bf16[28,2,1024]{2,1,0:T(2,128)(2,1)}, bf16[512,896]{1,0:T(8,128)(2,1)}) custom-call(bf16[128,1024]{1,0:T(8,128)(2,1)} %get-tuple-element.12.refs_0_, bf16[128,1024]{1,0:T(8,128)(2,1)} %get-tuple-element.13.refs_1_, bf16[28,2,1024]{2,1,0:T(2,128)(2,1)} %get-tuple-element.14.refs_2_, ...), custom_call_target="tpu_custom_call" | custom-call | tf_op jit(solution)/shard_map/settle/pallas_call | solution.py:604
